TPU v7x, 128 devices: a whole 4x4x4 slice. The times are simulated.
128 devices in a mesh: batch: 16 (over y, z_lo, core), seq: 8 (over x, z_hi).
Axes of the slice: x: 4, y: 4, z: 4 (z_hi: 2, z_lo: 2; z = z_hi * 2 + z_lo), core: 2. Of those that a mesh axis runs over, the one named last changes fastest.
Arguments:
- block_input: bfloat16 [16, 1024, 1536], P('batch', 'seq'), may hold values from -6 to 6
- doc_lengths: int32 [16, 6], P('batch'), may hold values from 1 to 1019, as said below
- ffn_levels: int32 [16, 6], P('batch'), may hold values from 0 to 3
- attn_gain: bfloat16 [1536], P(('batch', 'seq')), may hold values from 0.5 to 1.5
- qkv_weight: bfloat16 [1536, 4608], P(('batch', 'seq')), may hold values from -0.15625 to 0.15625
- out_weight: bfloat16 [1536, 1536], P(('batch', 'seq')), may hold values from -0.875 to 0.875
- ffn_gain: bfloat16 [1536], P(('batch', 'seq')), may hold values from 0.5 to 1.5
- up_weight: bfloat16 [1536, 6144], P(('batch', 'seq')), may hold values from -0.15625 to 0.15625
- down_weight: bfloat16 [6144, 1536], P(('batch', 'seq')), may hold values from -0.109375 to 0.109375
- grad_output: bfloat16 [16, 1024, 1536], P('batch', 'seq'), may hold values from -6 to 6
Outputs:
- block_output: bfloat16 [16, 1024, 1536], P('batch', 'seq')
- grad_input: float32 [16, 1024, 1536], P('batch', 'seq')
- grad_attn_gain: float32 [1536], P(('batch', 'seq'))
- grad_qkv: float32 [1536, 4608], P(('batch', 'seq'))
- grad_out: float32 [1536, 1536], P(('batch', 'seq'))
- grad_ffn_gain: float32 [1536], P(('batch', 'seq'))
- grad_up: float32 [1536, 6144], P(('batch', 'seq'))
- grad_down: float32 [6144, 1536], P(('batch', 'seq'))
Inputs may be any that keep to these rules, and one draw needn't show every extreme that they name: `doc_lengths`: in each group the 6 lengths sum to 1024; one of them, in a slot drawn from the seed, is longer than all the others together, and each of the others holds 1 to 16 tokens; in one group, drawn from the seed, each of the others holds exactly 1 token.
All inputs are finite; a program needn't handle non-finite values.
Results may differ from a plain program's by a relative error of at most 0.019.
Values may be sent and summed in bfloat16 or wider, within the bound.
A program may use at most 320 MiB of HBM per device.

v0:
```python
import math

import jax
import jax.numpy as jnp
import numpy as np
from jax import lax
from jax.experimental import pallas as pl
from jax.experimental.pallas import tpu as pltpu
from jax.sharding import PartitionSpec as P

HEADS = 12
HEAD_DIM = 128
D = 1536
FF = 6144
DOCS = 6
GROUP = 1024
SHARD = 128
RANK_HEADS = 3
RANK_COLS = 384
EPS = 1e-06
VMEM_LIMIT = 63 * 2**20
BF = jnp.bfloat16
F32 = jnp.float32
MESH = pl.DeviceIdType.MESH


def coords():
    b = lax.axis_index("batch")
    s = lax.axis_index("seq")
    return b // 4, (b // 2) % 2, b % 2, s // 2, s % 2


def dev(y, zl, c, x, zh):
    return (y * 4 + zl * 2 + c, x * 2 + zh)


def x_peers():
    y, zl, c, x, zh = coords()
    return [dev(y, zl, c, (x + k) % 4, zh) for k in (1, 2, 3)]


def y_peers():
    y, zl, c, x, zh = coords()
    return [dev((y + k) % 4, zl, c, x, zh) for k in (1, 2, 3)]


def z_peers():
    y, zl, c, x, zh = coords()
    z = zh * 2 + zl
    return [dev(y, (z + k) % 2, c, x, ((z + k) % 4) // 2) for k in (1, 2, 3)]


def core_peer():
    y, zl, c, x, zh = coords()
    return dev(y, zl, 1 - c, x, zh)


def zh_peer():
    y, zl, c, x, zh = coords()
    return dev(y, zl, c, x, 1 - zh)


class Lines:
    def __init__(self, send, recv):
        self.send, self.recv, self.used = send, recv, 0

    def copy(self, src, dst, peer):
        at = self.used
        self.used += 1
        return pltpu.make_async_remote_copy(
            src, dst, self.send.at[at], self.recv.at[at], device_id=peer, device_id_type=MESH
        )


LO, HI = pl.ds(0, 64), pl.ds(64, 64)


class RingGather:
    def __init__(self, lines, slot):
        self.lines, self.slot = lines, slot

    def start(self):
        x = coords()[3]
        nxt, _, prv = x_peers()
        lo, hi = self.slot(x).at[LO], self.slot(x).at[HI]
        self.first = self.lines.copy(lo, lo, nxt)
        self.second = self.lines.copy(hi, hi, prv)
        self.rest = [self.lines.copy(hi, hi, nxt), self.lines.copy(lo, lo, prv)]
        for cp in (self.first, self.second, *self.rest):
            cp.start()

    def on(self):
        x = coords()[3]
        nxt, _, prv = x_peers()
        lo, hi = self.slot((x + 3) % 4).at[LO], self.slot((x + 1) % 4).at[HI]
        self.first.wait_recv()
        one = self.lines.copy(lo, lo, nxt)
        one.start()
        self.second.wait_recv()
        two = self.lines.copy(hi, hi, prv)
        two.start()
        self.rest += [one, two]

    def finish(self):
        self.first.wait_send()
        self.second.wait_send()
        for cp in self.rest:
            cp.wait()


class RingScatter:
    def __init__(self, lines, part, got, via):
        self.lines, self.part, self.got, self.via = lines, part, got, via

    def start(self):
        x = coords()[3]
        nxt, _, prv = x_peers()
        left, right, far = (x + 3) % 4, (x + 1) % 4, (x + 2) % 4
        part = self.part
        self.far_lo = self.lines.copy(part(far).at[LO], self.via.at[0], nxt)
        self.far_hi = self.lines.copy(part(far).at[HI], self.via.at[1], prv)
        self.rest = [
            self.lines.copy(part(right).at[HI], self.got.at[2], nxt),
            self.lines.copy(part(left).at[LO], self.got.at[0], prv),
        ]
        for cp in (self.far_lo, self.far_hi, *self.rest):
            cp.start()

    def on(self):
        x = coords()[3]
        nxt, _, prv = x_peers()
        left, right = (x + 3) % 4, (x + 1) % 4
        via = self.via
        self.far_lo.wait_recv()
        via[0] = (via[0].astype(F32) + self.part(right)[LO].astype(F32)).astype(BF)
        one = self.lines.copy(via.at[0], self.got.at[1], nxt)
        one.start()
        self.far_hi.wait_recv()
        via[1] = (via[1].astype(F32) + self.part(left)[HI].astype(F32)).astype(BF)
        two = self.lines.copy(via.at[1], self.got.at[3], prv)
        two.start()
        self.rest += [one, two]

    def finish(self):
        self.far_lo.wait_send()
        self.far_hi.wait_send()
        for cp in self.rest:
            cp.wait()

    def total(self, own):
        got = self.got
        lo = got[0].astype(F32) + got[1].astype(F32)
        hi = got[2].astype(F32) + got[3].astype(F32)
        return own + jnp.concatenate([lo, hi], axis=0)


def one_hot_rows(rows, cols, expand):
    i = lax.broadcasted_iota(jnp.int32, (rows, cols), 0)
    j = lax.broadcasted_iota(jnp.int32, (rows, cols), 1)
    a, p = (j, i) if expand else (i, j)
    return jnp.where((p % 16 < 12) & (p // 16 * 12 + p % 16 == a), 1.0, 0.0).astype(BF)


def pick(matrix, values):
    return jnp.dot(matrix, values, preferred_element_type=F32).astype(BF)


def seq_peers():
    y, zl, c, x, zh = coords()
    s = x * 2 + zh
    found = []
    for k in range(1, 8):
        t = (s + k) % 8
        found.append(dev(y, zl, c, t // 2, t % 2))
    return found


def greet():
    y, _, _, x, _ = coords()
    sem = pltpu.get_barrier_semaphore()
    peers = seq_peers() + y_peers() + z_peers()[::2] + [core_peer()]
    for peer in peers:
        pl.semaphore_signal(sem, inc=1, device_id=peer, device_id_type=MESH)

    @pl.when(x != y)
    def _():
        pl.semaphore_signal(sem, inc=1, device_id=swap_xy(), device_id_type=MESH)

    return len(peers) + jnp.where(x != y, 1, 0)


def swap_xy():
    y, zl, c, x, zh = coords()
    return dev(x, zl, c, y, zh)


def spread(lines, src, dst):
    y, zl, c, x, zh = coords()
    s = x * 2 + zh
    at = lines.used
    lines.used += 4
    sends, arrivals = [], []
    for k in range(4):
        i = (x + k) % 4
        own = (i == x) & (x // 2 == zh)
        cp = pltpu.make_async_remote_copy(
            src.at[i], dst.at[s % 4], lines.send.at[at + k], lines.recv.at[at + s % 4],
            device_id=dev(y, zl, c, i, x // 2), device_id_type=MESH,
        )
        sends.append((cp, own))
    for j in range(4):
        own = (x // 2 == zh) & (s % 4 == j)
        cp = pltpu.make_async_remote_copy(
            src.at[j], dst.at[j], lines.send.at[at], lines.recv.at[at + j],
            device_id=core_peer(), device_id_type=MESH,
        )
        arrivals.append((cp, own))
    return sends, arrivals, (x // 2 == zh), x, s % 4


def gather_home(lines, src, dst):
    y, zl, c, x, zh = coords()
    s = x * 2 + zh
    at = lines.used
    lines.used += 4
    sends, arrivals = [], []
    for k in range(4):
        i = (s + k) % 4
        t = 4 * zh + i
        own = t == s
        cp = pltpu.make_async_remote_copy(
            src.at[i], dst.at[x], lines.send.at[at + k], lines.recv.at[at + x],
            device_id=dev(y, zl, c, t // 2, t % 2), device_id_type=MESH,
        )
        sends.append((cp, own))
    for j in range(4):
        own = (x // 2 == zh) & (x == j)
        cp = pltpu.make_async_remote_copy(
            src.at[j], dst.at[j], lines.send.at[at], lines.recv.at[at + j],
            device_id=core_peer(), device_id_type=MESH,
        )
        arrivals.append((cp, own))
    return sends, arrivals, (x // 2 == zh), s % 4, x


def start_all(plan, src, dst):
    sends, _, mine, from_slot, to_slot = plan
    for cp, own in sends:
        pl.when(jnp.logical_not(own))(cp.start)

    @pl.when(mine)
    def _():
        dst[to_slot] = src[from_slot]


def wait_all(plan):
    sends, arrivals = plan[:2]
    for cp, own in arrivals:
        pl.when(jnp.logical_not(own))(cp.wait_recv)
    for cp, own in sends:
        pl.when(jnp.logical_not(own))(cp.wait_send)


class Gather:
    def __init__(self, lines, full, rows, z_first, y_inner=False, columns=None):
        self.lines, self.full, self.rows, self.z_first, self.y_inner = lines, full, rows, z_first, y_inner
        self.columns = pl.ds(0, full.shape[-1]) if columns is None else columns
        self.pending = []

    def _at(self, y, zl, c, rows):
        place = (zl, c, y) if self.y_inner else (y, zl, c)
        return self.full.at[(*place, rows, self.columns)]

    def _send(self, src, peers):
        copies = [self.lines.copy(src, src, p) for p in peers]
        for cp in copies:
            cp.start()
        self.pending = copies

    def near(self):
        y, zl, c, _, zh = coords()
        mine = self._at(y, zl, c, pl.ds(zh * self.rows, self.rows))
        self._send(mine, z_peers() if self.z_first else y_peers())

    def wide(self):
        self.wait()
        y, zl, c, _, zh = coords()
        if self.z_first:
            self._send(self._at(y, slice(None), c, pl.ds(0, 2 * self.rows)), y_peers())
        else:
            self._send(self._at(slice(None), zl, c, pl.ds(zh * self.rows, self.rows)), z_peers())

    def cores(self):
        self.wait()
        c = coords()[2]
        self._send(self._at(slice(None), slice(None), c, pl.ds(0, 2 * self.rows)), [core_peer()])

    def wait(self):
        for cp in self.pending:
            cp.wait()
        self.pending = []


class Scatter:
    def __init__(self, lines, part, bufs, rows, y_first, y_inner=False, columns=None):
        self.lines, self.part = lines, part
        self.half, self.near_in, self.wide, self.wide_in = bufs
        self.rows, self.y_first, self.y_inner, self.pending = rows, y_first, y_inner, []
        self.columns = pl.ds(0, part.shape[-1]) if columns is None else columns

    def wait(self):
        for cp in self.pending:
            cp.wait()
        self.pending = []

    def _start(self, copies):
        for cp in copies:
            cp.start()
        self.pending = copies

    def cores(self):
        c = coords()[2]
        rows = pl.ds(0, 2 * self.rows)
        place = (slice(None), 1 - c, slice(None)) if self.y_inner else (slice(None), slice(None), 1 - c)
        self._start([self.lines.copy(self.part.at[(*place, rows, self.columns)], self.half, core_peer())])

    def first(self):
        self.wait()
        y, zl, c, _, zh = coords()
        z, rows, inner = zh * 2 + zl, self.rows, self.half.shape[1]

        @pl.loop(0, 8)
        def _(i):
            a, b = i // inner, i % inner
            place = (a, c, b) if self.y_inner else (a, b, c)
            both = self.part[(*place, slice(None), self.columns)].astype(F32) + self.half[a, b].astype(F32)
            self.half[a, b] = both.astype(BF)

        copies = []
        for k in (1, 2, 3):
            if self.y_first:
                yy = (y + k) % 4
                src, peer = self.half.at[:, yy] if self.y_inner else self.half.at[yy], y_peers()[k - 1]
            else:
                zz = (z + k) % 4
                src, peer = self.half.at[:, zz % 2, pl.ds(zz // 2 * rows, rows)], z_peers()[k - 1]
            copies.append(self.lines.copy(src, self.near_in.at[k - 1], peer))
        self._start(copies)

    def second(self):
        self.wait()
        y, zl, c, _, zh = coords()
        z, rows = zh * 2 + zl, self.rows
        copies = []
        for i in range(self.wide.shape[0]):
            if self.y_first:
                total = (self.half[i, y] if self.y_inner else self.half[y, i]).astype(F32)
            else:
                total = self.half[i, zl, pl.ds(zh * rows, rows)].astype(F32)
            for k in range(3):
                total += self.near_in[k, i].astype(F32)
            self.wide[i] = total.astype(BF)
        for k in (1, 2, 3):
            if self.y_first:
                zz = (z + k) % 4
                src, peer = self.wide.at[zz % 2, pl.ds(zz // 2 * rows, rows)], z_peers()[k - 1]
            else:
                src, peer = self.wide.at[(y + k) % 4], y_peers()[k - 1]
            copies.append(self.lines.copy(src, self.wide_in.at[k - 1], peer))
        self._start(copies)

    def total(self):
        self.wait()
        y, zl, c, _, zh = coords()
        if self.y_first:
            total = self.wide[zl, pl.ds(zh * self.rows, self.rows)].astype(F32)
        else:
            total = self.wide[y].astype(F32)
        for k in range(3):
            total += self.wide_in[k].astype(F32)
        return total


def scatter_scratch(rows, n, y_first, y_inner=False):
    half = pltpu.VMEM((2, 4, 2 * rows, n) if y_inner else (4, 2, 2 * rows, n), BF)
    if y_first:
        near_in, wide = pltpu.VMEM((3, 2, 2 * rows, n), BF), pltpu.VMEM((2, 2 * rows, n), BF)
    else:
        near_in, wide = pltpu.VMEM((3, 4, rows, n), BF), pltpu.VMEM((4, rows, n), BF)
    return [half, near_in, wide, pltpu.VMEM((3, rows, n), BF)]


def dot(a, b):
    return jnp.dot(a, b, preferred_element_type=F32)


def dot_nt(a, b):
    return lax.dot_general(a, b, (((1,), (1,)), ((), ())), preferred_element_type=F32)


def dot_tn(a, b):
    return lax.dot_general(a, b, (((0,), (0,)), ((), ())), preferred_element_type=F32)


def normalize(values):
    r = lax.rsqrt(jnp.mean(values * values, axis=-1, keepdims=True) + EPS)
    return r, values * r


def rms_back(grad, values):
    r, hat = normalize(values)
    return r * (grad - hat * jnp.mean(grad * hat, axis=-1, keepdims=True))


def cos_sin(table):
    other = pltpu.roll(table, 64, 1)
    low = lax.broadcasted_iota(jnp.int32, table.shape, 1) < 64
    return jnp.where(low, table, other), jnp.where(low, -other, table)


def turn(v, cos, sin):
    return v * cos + pltpu.roll(v, 64, 1) * sin


def turn_back(v, cos, sin):
    return v * cos - pltpu.roll(v, 64, 1) * sin


GELU_A, GELU_B = math.sqrt(2.0 / math.pi), 0.044715


def gelu_both(v):
    square = v * v
    t = jnp.tanh(GELU_A * v * (1.0 + GELU_B * square))
    half = 0.5 * (1.0 + t)
    return v * half, half + 0.5 * v * (1.0 - t * t) * (GELU_A * (1.0 + 3.0 * GELU_B * square))


def cols(i, n):
    return pl.ds(pl.multiple_of(i * n, n), n)


NAMES = (
    "full_q", "full_u", "full_d", "full_o", "got_q", "got_u", "src_q", "src_u", "src_o",
    "normed", "q_ref", "k_ref", "v_ref", "p0", "p1", "p2", "p3",
    "att", "att_grad", "middle", "wo", "ntwo", "up_grad", "hidden", "pre_grad", "branch", "part_a", "part_c",
    "got_a", "via_a", "got_b", "via_b", "got_c", "via_c", "swap_out", "swap_in", "dk_t", "dv_t",
    "sq0", "sq1", "sq2", "sq3", "sr0", "sr1", "sr2", "sr3", "su0", "su1", "su2", "su3",
    "sd0", "sd1", "sd2", "sd3", "so0", "so1", "so2", "so3", "fin_o", "fin_d", "send", "recv",
)


def scratch_list():
    V = pltpu.VMEM
    block = V((4, 128, D), BF)
    got, via = V((4, 64, D), BF), V((2, 64, D), BF)
    kv = V((3, 4, 2, 128, 128), BF)
    shapes = [V((4, 2, 2, 96, 1152), BF), V((4, 2, 2, 96, D), BF), V((2, 2, 4, 96, D), BF), V((2, 2, 4, 32, D), BF)]
    shapes += [V((4, 16, 1152), BF), V((4, 16, D), BF)] * 2 + [V((16, D), BF)]
    shapes += [V((4, 2, 128, D), BF), V((3, 4, 128, 128), BF), kv, kv]
    shapes += [V((3, 128, 256 * (i + 1)), BF) for i in range(4)]
    shapes += [V((4, 128, RANK_COLS), BF), V((4, 128, RANK_COLS), BF), V((128, D), F32), V((RANK_COLS, D), BF)]
    shapes += [block] * 7
    shapes += [got, via] * 3 + [V((128, D), BF), V((128, D), BF)]
    shapes += [V((128, GROUP), F32), V((128, GROUP), F32)]
    shapes += scatter_scratch(48, 640, False) + scatter_scratch(48, 512, True) + scatter_scratch(48, D, False)
    shapes += scatter_scratch(48, D, True, True) + scatter_scratch(16, D, True, True)
    shapes += [V((16, D), BF), V((48, D), BF)]
    shapes += [pltpu.SemaphoreType.DMA((160,)), pltpu.SemaphoreType.DMA((160,))]
    assert len(shapes) == len(NAMES)
    return shapes


class Refs:
    pass


def column(row):
    n = row.shape[1]
    same = lax.broadcasted_iota(jnp.int32, (n, n), 0) == lax.broadcasted_iota(jnp.int32, (n, n), 1)
    return jnp.sum(jnp.where(same, row, 0.0), axis=1, keepdims=True)


def as_row(col):
    n = col.shape[0]
    same = lax.broadcasted_iota(jnp.int32, (n, n), 0) == lax.broadcasted_iota(jnp.int32, (n, n), 1)
    return jnp.sum(jnp.where(same, col, 0.0), axis=0, keepdims=True)


def sixteen(rows):
    return jnp.concatenate([rows, jnp.zeros((4, rows.shape[1]), rows.dtype)], axis=0).astype(BF)


def documents(lengths, levels, positions):
    start, width = jnp.zeros_like(positions), jnp.zeros_like(positions)
    first = 0
    for d in range(DOCS):
        level = levels[0, d]
        wide = jnp.where(level == 0, FF // 8, jnp.where(level == 1, FF // 4, jnp.where(level == 2, FF // 2, FF)))
        inside = positions >= first
        start = jnp.where(inside, first, start)
        width = jnp.where(inside, wide, width)
        first = first + lengths[0, d]
    return start, width


def layer_kernel(
    lengths, levels, tokens, grad_in, qkv, out_w, up, down, gain_one, gain_two, angles,
    block_out, grad_input, out_q, out_u, out_d, out_o, *scratch
):
    g = Refs()
    for name, ref in zip(NAMES, scratch):
        setattr(g, name, ref)
    y, zl, c, x, zh = coords()
    lines = Lines(g.send, g.recv)
    scale = HEAD_DIM**-0.5
    greetings = greet()

    g.normed[x, zh] = normalize(tokens[...].astype(F32))[1].astype(BF)
    g.up_grad[x] = grad_in[...]
    one, two = column(gain_one[...].astype(F32)), column(gain_two[...].astype(F32))
    for i in range(4):
        for j in range(3):
            at = j * D + i * RANK_COLS
            g.src_q[i, :, j * RANK_COLS : (j + 1) * RANK_COLS] = sixteen(qkv[:, at : at + RANK_COLS].astype(F32) * one)
        g.src_u[i] = sixteen(up[:, i * D : (i + 1) * D].astype(F32) * two)
    g.src_o[...] = sixteen(out_w[...].astype(F32))
    pl.semaphore_wait(pltpu.get_barrier_semaphore(), greetings)

    ring_one = RingGather(lines, lambda i: g.normed.at[i, zh])
    ring_two = RingGather(lines, lambda i: g.normed.at[i, 1 - zh])
    swap = lines.copy(g.normed.at[x, zh], g.normed.at[x, zh], zh_peer())
    plan_q = spread(lines, g.src_q, g.got_q)
    start_all(plan_q, g.src_q, g.got_q)
    ring_one.start()
    swap.start()
    plan_u = spread(lines, g.src_u, g.got_u)
    start_all(plan_u, g.src_u, g.got_u)
    swap_o = lines.copy(g.src_o, g.full_o.at[zl, c, x, pl.ds(zh * 16, 16)], swap_xy())
    swap_d = lines.copy(down, g.full_d.at[zl, c, x, pl.ds(zh * 48, 48)], swap_xy())

    @pl.when(x != y)
    def _():
        swap_o.start()
        swap_d.start()

    @pl.when(x == y)
    def _():
        g.full_o[zl, c, x, pl.ds(zh * 16, 16)] = g.src_o[...]
        g.full_d[zl, c, x, pl.ds(zh * 48, 48)] = down[...]

    rows = one_hot_rows(48, 64, False)
    wait_all(plan_q)
    g.full_q[y, zl, c, pl.ds(zh * 48, 48)] = pick(rows, g.got_q[...].reshape(64, 1152))
    gather_q = [
        Gather(lines, g.full_q, 48, True, False, pl.ds(0, 640)),
        Gather(lines, g.full_q, 48, False, False, pl.ds(640, 512)),
    ]
    for t in gather_q:
        t.near()
    ring_one.on()
    for t in gather_q:
        t.wide()
    gather_o = Gather(lines, g.full_o, 16, False, True)
    gather_u = Gather(lines, g.full_u, 48, True)
    gather_d = Gather(lines, g.full_d, 48, False, True)

    @pl.when(x != y)
    def _():
        swap_o.wait()
        swap_d.wait()

    gather_o.near()
    swap.wait_recv()
    ring_two.start()
    wait_all(plan_u)
    g.full_u[y, zl, c, pl.ds(zh * 48, 48)] = pick(rows, g.got_u[...].reshape(64, D))
    gather_d.near()
    gather_u.near()
    ring_one.finish()
    for t in gather_q:
        t.cores()
    gather_o.wide()
    ring_two.on()
    for t in gather_q:
        t.wait()

    def project(zz, own_half):
        block = g.normed[:, zz].reshape(512, D)
        cos_b, sin_b = cos_sin(angles[:, zz].reshape(512, 128))
        for j in range(0 if own_half else 1, 3):
            made = dot(block, g.full_q[:, :, :, :, j * RANK_COLS : (j + 1) * RANK_COLS].reshape(D, RANK_COLS))
            for h in range(RANK_HEADS):
                head = made[:, h * 128 : (h + 1) * 128]
                if j < 2:
                    head = turn(head, cos_b, sin_b)
                head = head.astype(BF).reshape(4, 128, 128)
                if j == 0:
                    g.q_ref[h] = head
                elif j == 1:
                    g.k_ref[h, :, zz] = head
                else:
                    g.v_ref[h, :, zz] = head

    project(zh, True)
    ring_two.finish()
    swap.wait_send()
    ring_up = RingGather(lines, lambda i: g.up_grad.at[i])
    ring_up.start()
    gather_d.wide()
    gather_u.wide()
    project(1 - zh, False)
    gather_o.cores()

    probs = [g.p0, g.p1, g.p2, g.p3]

    @pl.loop(0, RANK_HEADS)
    def _(h):
        for i in range(4):
            n = 256 * (i + 1)
            keys = g.k_ref[h, : i + 1].reshape(n, 128)
            values = g.v_ref[h, : i + 1].reshape(n, 128)
            scores = dot_nt(g.q_ref[h, i], keys) * scale
            base = (2 * i + zh) * 128
            q_at = base + lax.broadcasted_iota(jnp.int32, (128, n), 0)
            k_at = lax.broadcasted_iota(jnp.int32, (128, n), 1)
            first = documents(lengths, levels, base + lax.broadcasted_iota(jnp.int32, (128, 1), 0))[0]
            scores = jnp.where((k_at <= q_at) & (k_at >= first), scores, -1e30)
            e = jnp.exp(scores - jnp.max(scores, axis=-1, keepdims=True))
            p = (e * (1.0 / jnp.sum(e, axis=-1, keepdims=True))).astype(BF)
            probs[i][h] = p
            g.att[i, :, pl.ds(pl.multiple_of(h * 128, 128), 128)] = dot(p, values).astype(BF)

    ring_up.on()
    gather_o.wait()
    g.wo[...] = pick(one_hot_rows(RANK_COLS, 512, False), g.full_o[...].reshape(512, D))

    def to_parts(parts, left, right_of, transposed, tiles):
        n = D // tiles

        @pl.loop(0, tiles)
        def _(t):
            right = right_of(t)
            made = dot_nt(left, right) if transposed else dot(left, right)
            parts[:, :, cols(t, n)] = made.astype(BF).reshape(4, 128, n)

    to_parts(g.part_a, g.att[...].reshape(512, RANK_COLS), lambda t: g.wo[:, cols(t, 512)], False, 3)
    ring_a = RingScatter(lines, lambda i: g.part_a.at[i], g.got_a, g.via_a)
    ring_a.start()
    ring_up.finish()
    ring_a.on()
    ring_a.finish()
    g.middle[...] = ring_a.total(tokens[...].astype(F32) + g.part_a[x].astype(F32))
    g.ntwo[x] = normalize(g.middle[...])[1].astype(BF)
    ring_n = RingGather(lines, lambda i: g.ntwo.at[i])
    ring_n.start()
    gather_d.cores()
    gather_u.cores()
    ring_n.on()

    def full_rows(ref, t):
        return ref[pl.ds(t * 2, 2)].reshape(768, ref.shape[-1])

    def full_cols(ref, t, n):
        return ref[:, :, :, :, cols(t, n)].reshape(D, n)

    gather_d.wait()
    up_all = g.up_grad[...].reshape(512, D)
    to_parts(g.pre_grad, up_all, lambda t: g.full_d[t].reshape(768, D), True, 2)
    gather_u.wait()
    ring_n.finish()

    width = jnp.concatenate(
        [
            documents(lengths, levels, (2 * i + zh) * 128 + lax.broadcasted_iota(jnp.int32, (128, 1), 0))[1]
            for i in range(4)
        ],
        axis=0,
    )

    @pl.loop(0, 6)
    def _(t):
        pre = dot(g.ntwo[...].reshape(512, D), full_cols(g.full_u, t, 256))
        unit = x * D + t * 256 + lax.broadcasted_iota(jnp.int32, (512, 256), 1)
        mask = unit < width
        act, slope = gelu_both(pre)
        g.hidden[:, :, cols(t, 256)] = jnp.where(mask, act, 0.0).astype(BF).reshape(4, 128, 256)
        back = g.pre_grad[:, :, cols(t, 256)].reshape(512, 256).astype(F32)
        g.pre_grad[:, :, cols(t, 256)] = jnp.where(mask, slope * back, 0.0).astype(BF).reshape(4, 128, 256)

    pre_all = g.pre_grad[...].reshape(512, D)
    to_parts(g.part_a, pre_all, lambda t: full_rows(g.full_u, t), True, 2)
    ring_b = RingScatter(lines, lambda i: g.part_a.at[i], g.got_b, g.via_b)
    ring_b.start()

    def weight_grad(full, left_of, right):
        @pl.loop(0, 4)
        def _(t):
            made = dot_tn(left_of(t), right).astype(BF)
            if full.shape[0] == 4:
                full[t] = made.reshape(full.shape[1:])
            else:
                full[t // 2, t % 2] = made.reshape(full.shape[2:])

    weight_grad(g.full_u, lambda t: g.ntwo[:, :, cols(t, 384)].reshape(512, 384), pre_all)
    scatter_u = Scatter(lines, g.full_u, (g.su0, g.su1, g.su2, g.su3), 48, False)
    scatter_u.cores()
    ring_b.on()
    to_parts(g.part_c, g.hidden[...].reshape(512, D), lambda t: full_cols(g.full_d, t, 512), False, 3)
    scatter_u.first()
    weight_grad(g.full_d, lambda t: g.hidden[:, :, cols(t, 384)].reshape(512, 384), up_all)
    scatter_d = Scatter(lines, g.full_d, (g.sd0, g.sd1, g.sd2, g.sd3), 48, True, True)
    scatter_d.cores()
    ring_b.finish()

    grad_input[...] = grad_in[...].astype(F32) + rms_back(ring_b.total(g.part_a[x].astype(F32)), g.middle[...])
    g.branch[x] = grad_input[...].astype(BF)
    ring_g = RingGather(lines, lambda i: g.branch.at[i])
    ring_g.start()
    scatter_d.first()
    ring_g.on()
    ring_g.finish()
    ring_c = RingScatter(lines, lambda i: g.part_c.at[i], g.got_c, g.via_c)
    ring_c.start()

    branch_all = g.branch[...].reshape(512, D)
    g.att_grad[...] = dot_nt(branch_all, g.wo[...]).astype(BF).reshape(4, 128, RANK_COLS)

    @pl.loop(0, RANK_HEADS)
    def _(h):
        at = pl.ds(pl.multiple_of(h * 128, 128), 128)
        g.dk_t[...] = jnp.zeros_like(g.dk_t)
        g.dv_t[...] = jnp.zeros_like(g.dv_t)
        for i in range(4):
            n = 256 * (i + 1)
            keys = g.k_ref[h, : i + 1].reshape(n, 128)
            values = g.v_ref[h, : i + 1].reshape(n, 128)
            queries = g.q_ref[h, i]
            p = probs[i][h]
            grad = g.att_grad[i, :, at]
            delta = jnp.sum(grad.astype(F32) * g.att[i, :, at].astype(F32), axis=-1, keepdims=True)
            ds = (p.astype(F32) * (dot_nt(grad, values) - delta)).astype(BF)
            dq = dot(ds, keys) * scale
            g.dk_t[:, :n] += dot(queries.T, ds)
            g.dv_t[:, :n] += dot(grad.T, p)
            g.q_ref[h, i] = turn_back(dq, *cos_sin(angles[i, zh])).astype(BF)
        dk = g.dk_t[...].T * scale
        dk = turn_back(dk, *cos_sin(angles[...].reshape(GROUP, 128)))
        g.k_ref[h] = dk.astype(BF).reshape(4, 2, 128, 128)
        g.v_ref[h] = g.dv_t[...].T.astype(BF).reshape(4, 2, 128, 128)

    ring_c.on()

    def side(ref, zz):
        return [ref[h, :, zz].reshape(512, 128) for h in range(RANK_HEADS)]

    def first_parts(parts, zz, own_half):
        pieces = side(g.k_ref, zz) + side(g.v_ref, zz)
        if own_half:
            pieces = [g.q_ref[h].reshape(512, 128) for h in range(RANK_HEADS)] + pieces
        left = jnp.concatenate(pieces, axis=1)
        n = left.shape[1]
        to_parts(parts, left, lambda t: g.full_q[pl.ds(t * 2, 2), :, :, :, 1152 - n :].reshape(768, n), True, 2)

    first_parts(g.part_a, 1 - zh, False)
    ring_e = RingScatter(lines, lambda i: g.part_a.at[i], g.got_a, g.via_a)
    ring_e.start()
    scatter_u.second()
    ring_c.finish()
    block_out[...] = ring_c.total(g.middle[...] + g.part_c[x].astype(F32)).astype(BF)
    first_parts(g.part_c, zh, True)
    ring_f = RingScatter(lines, lambda i: g.part_c.at[i], g.got_b, g.via_b)
    ring_f.start()

    dq_all = jnp.concatenate([g.q_ref[h].reshape(512, 128) for h in range(RANK_HEADS)], axis=1)
    dkv_all = jnp.concatenate(
        [r[h].reshape(GROUP, 128) for r in (g.k_ref, g.v_ref) for h in range(RANK_HEADS)], axis=1
    )

    @pl.loop(0, 4)
    def _(t):
        mine = g.normed[:, zh, :, cols(t, 384)].reshape(512, 384)
        every = g.normed[:, :, :, cols(t, 384)].reshape(GROUP, 384)
        g.full_q[t, :, :, :, :RANK_COLS] = dot_tn(mine, dq_all).astype(BF).reshape(2, 2, 96, RANK_COLS)
        g.full_q[t, :, :, :, RANK_COLS:] = dot_tn(every, dkv_all).astype(BF).reshape(2, 2, 96, 768)

    scatter_q = [
        Scatter(lines, g.full_q, (g.sq0, g.sq1, g.sq2, g.sq3), 48, False, False, pl.ds(0, 640)),
        Scatter(lines, g.full_q, (g.sr0, g.sr1, g.sr2, g.sr3), 48, True, False, pl.ds(640, 512)),
    ]
    for t in scatter_q:
        t.cores()
    ring_e.on()
    scatter_d.second()
    d_out = dot_tn(g.att[...].reshape(512, RANK_COLS), branch_all).astype(BF)
    g.full_o[...] = pick(one_hot_rows(512, RANK_COLS, True), d_out).reshape(2, 2, 4, 32, D)
    scatter_o = Scatter(lines, g.full_o, (g.so0, g.so1, g.so2, g.so3), 16, True, True)
    scatter_o.cores()
    for t in scatter_q:
        t.first()
    ring_f.on()
    scatter_o.first()
    ring_e.finish()
    g.swap_out[...] = ring_e.total(g.part_a[x].astype(F32)).astype(BF)
    back = lines.copy(g.swap_out, g.swap_in, zh_peer())
    back.start()

    spread_rows = one_hot_rows(64, 48, True)
    g.got_u[...] = pick(spread_rows, scatter_u.total().astype(BF)).reshape(4, 16, D)
    plan_u = gather_home(lines, g.got_u, out_u)
    start_all(plan_u, g.got_u, out_u)
    for t in scatter_q:
        t.second()
    scatter_o.second()
    g.fin_d[...] = scatter_d.total().astype(BF)
    home_d = lines.copy(g.fin_d, out_d, swap_xy())
    home_o = lines.copy(g.fin_o, out_o, swap_xy())
    pl.when(x != y)(home_d.start)
    ring_f.finish()
    back.wait()
    h_one = ring_f.total(g.part_c[x].astype(F32)) + g.swap_in[...].astype(F32)
    grad_input[...] += rms_back(h_one, tokens[...].astype(F32))
    both = jnp.concatenate([scatter_q[0].total().astype(BF), scatter_q[1].total().astype(BF)], axis=1)
    g.got_q[...] = pick(spread_rows, both).reshape(4, 16, 1152)
    plan_q = gather_home(lines, g.got_q, out_q)
    start_all(plan_q, g.got_q, out_q)
    g.fin_o[...] = scatter_o.total().astype(BF)
    pl.when(x != y)(home_o.start)

    @pl.when(x == y)
    def _():
        out_o[...] = g.fin_o[...]
        out_d[...] = g.fin_d[...]

    wait_all(plan_u)

    @pl.when(x != y)
    def _():
        home_d.wait()
        home_o.wait()

    wait_all(plan_q)


def finish_kernel(
    block, grad, got_q, got_u, got_d, got_o, qkv, up, gain_one, gain_two,
    block_out, grad_input, d_gain_one, d_qkv, d_out, d_gain_two, d_up, d_down
):
    block_out[...] = block[...]
    grad_input[...] = grad[...]
    d_down[...] = got_d[...].astype(F32)
    d_out[...] = got_o[:12].astype(F32)
    one, two = column(gain_one[...].astype(F32)), column(gain_two[...].astype(F32))
    sum_one = sum_two = jnp.zeros((12, 1), F32)
    for i in range(4):
        for j in range(3):
            raw = got_q[i, :12, j * RANK_COLS : (j + 1) * RANK_COLS].astype(F32)
            at = j * D + i * RANK_COLS
            sum_one += jnp.sum(raw * qkv[:, at : at + RANK_COLS].astype(F32), axis=1, keepdims=True)
            d_qkv[:, at : at + RANK_COLS] = raw * one
        raw = got_u[i, :12].astype(F32)
        sum_two += jnp.sum(raw * up[:, i * D : (i + 1) * D].astype(F32), axis=1, keepdims=True)
        d_up[:, i * D : (i + 1) * D] = raw * two
    d_gain_one[...] = as_row(sum_one)
    d_gain_two[...] = as_row(sum_two)


def tables():
    inverse = np.exp(np.arange(64) * (-2.0 * math.log(10000.0) / HEAD_DIM))
    angles = np.arange(GROUP)[:, None] * inverse[None, :]
    return np.concatenate([np.cos(angles), np.sin(angles)], axis=1).astype(np.float32).reshape(4, 2, 128, 128)


def shapes_of(pairs):
    return [jax.ShapeDtypeStruct(s, t) for s, t in pairs]


def per_device(
    block_input, doc_lengths, ffn_levels, attn_gain, qkv_weight, out_weight, ffn_gain, up_weight, down_weight, grad_output
):
    vmem = pl.BlockSpec(memory_space=pltpu.VMEM)
    smem = pl.BlockSpec(memory_space=pltpu.SMEM)
    gain_one, gain_two = attn_gain.reshape(1, 12), ffn_gain.reshape(1, 12)
    outs = [((128, D), BF), ((128, D), F32), ((4, 16, 1152), BF), ((4, 16, D), BF), ((48, D), BF), ((16, D), BF)]
    made = pl.pallas_call(
        layer_kernel,
        out_shape=shapes_of(outs),
        in_specs=[smem] * 2 + [vmem] * 9,
        out_specs=[vmem] * len(outs),
        scratch_shapes=scratch_list(),
        compiler_params=pltpu.CompilerParams(collective_id=0, has_side_effects=True, vmem_limit_bytes=VMEM_LIMIT),
        name="layer_kernel",
    )(
        doc_lengths, ffn_levels, block_input[0], grad_output[0], qkv_weight, out_weight, up_weight, down_weight,
        gain_one, gain_two, jnp.asarray(tables()),
    )
    outs = [((128, D), BF), ((128, D), F32), ((1, 12), F32), ((12, 3 * D), F32), ((12, D), F32), ((1, 12), F32)]
    outs += [((12, FF), F32), ((48, D), F32)]
    block, grad, d_gain_one, d_qkv, d_out, d_gain_two, d_up, d_down = pl.pallas_call(
        finish_kernel,
        out_shape=shapes_of(outs),
        in_specs=[vmem] * 10,
        out_specs=[vmem] * len(outs),
        compiler_params=pltpu.CompilerParams(vmem_limit_bytes=VMEM_LIMIT),
        name="finish_kernel",
    )(*made, qkv_weight, up_weight, gain_one, gain_two)
    return block[None], grad[None], d_gain_one.reshape(12), d_qkv, d_out, d_gain_two.reshape(12), d_up, d_down


def solution(mesh):
    rows = P("batch", "seq", None)
    every = ("batch", "seq")
    return jax.shard_map(
        per_device,
        mesh=mesh,
        in_specs=(rows, P("batch", None), P("batch", None), P(every), P(every, None), P(every, None), P(every),
                  P(every, None), P(every, None), rows),
        out_specs=(rows, rows, P(every), P(every, None), P(every, None), P(every), P(every, None), P(every, None)),
        check_vma=False,
    )
```

profile of v0, /device:TPU:0, one launch (start us, length us, event | category | flops | bytes accessed | tf_op | source)
XLA Modules:
  0.0 213.6 jit_solution(12217821093096111047)
XLA Ops:
  0.6 209.9 %layer_kernel.1 = (bf16[128,1536]{1,0:T(8,128)(2,1)}, f32[128,1536]{1,0:T(8,128)}, bf16[4,16,1152]{2,1,0:T(8,128)(2,1)}, bf16[4,16,1536]{2,1,0:T(8,128)(2,1)}, b...) custom-call(s32[1,6]{1,0:T(1,128)} %lengths.1, s32[1,6]{1,0:T(1,128)} %levels.1, bf16[128,1536]{1,0:T(8,128)(2,1)} %bitcast.8, ...), custom_call_target="tpu_custom_call" | custom-call | tf_op jit(solution)/shard_map/layer_kernel/pallas_call | solution.py:885
  210.6 3.1 %finish_kernel.1 = (bf16[128,1536]{1,0:T(8,128)(2,1)}, f32[128,1536]{1,0:T(8,128)}, f32[1,12]{1,0:T(1,128)}, f32[12,4608]{1,0:T(8,128)}, f32[12,1536]{1,0:T(8,12...) custom-call(bf16[128,1536]{1,0:T(8,128)(2,1)} %get-tuple-element.22.block, ...), custom_call_target="tpu_custom_call" | custom-call | tf_op jit(solution)/shard_map/finish_kernel/pallas_call | solution.py:899
where the time goes:
time: 215 us; the launch traced here: 214 us
  Pallas kernels  213 us (99%)
    pallas_call x1, Pallas kernels, per_device(): pl.pallas_call(layer_kernel, out_shape=shapes_of(outs), in_specs=[smem] *...  210 us

commit v1 on v0

--- a/solution.py
+++ b/solution.py
@@ -75,14 +75,22 @@
 LO, HI = pl.ds(0, 64), pl.ds(64, 64)
 
 
+def ring(axis):
+    y, zl, c, x, zh = coords()
+    if axis == "x":
+        return x, x_peers()[0], x_peers()[2]
+    if axis == "y":
+        return y, y_peers()[0], y_peers()[2]
+    return zh * 2 + zl, z_peers()[0], z_peers()[2]
+
+
 class RingGather:
-    def __init__(self, lines, slot):
-        self.lines, self.slot = lines, slot
+    def __init__(self, lines, axis, lo, hi):
+        self.lines, self.axis, self.lo, self.hi = lines, axis, lo, hi
 
     def start(self):
-        x = coords()[3]
-        nxt, _, prv = x_peers()
-        lo, hi = self.slot(x).at[LO], self.slot(x).at[HI]
+        me, nxt, prv = ring(self.axis)
+        lo, hi = self.lo(me), self.hi(me)
         self.first = self.lines.copy(lo, lo, nxt)
         self.second = self.lines.copy(hi, hi, prv)
         self.rest = [self.lines.copy(hi, hi, nxt), self.lines.copy(lo, lo, prv)]
@@ -90,9 +98,8 @@
             cp.start()
 
     def on(self):
-        x = coords()[3]
-        nxt, _, prv = x_peers()
-        lo, hi = self.slot((x + 3) % 4).at[LO], self.slot((x + 1) % 4).at[HI]
+        me, nxt, prv = ring(self.axis)
+        lo, hi = self.lo((me + 3) % 4), self.hi((me + 1) % 4)
         self.first.wait_recv()
         one = self.lines.copy(lo, lo, nxt)
         one.start()
@@ -109,34 +116,31 @@
 
 
 class RingScatter:
-    def __init__(self, lines, part, got, via):
-        self.lines, self.part, self.got, self.via = lines, part, got, via
+    def __init__(self, lines, axis, lo, hi, got, via):
+        self.lines, self.axis, self.lo, self.hi, self.got, self.via = lines, axis, lo, hi, got, via
 
     def start(self):
-        x = coords()[3]
-        nxt, _, prv = x_peers()
-        left, right, far = (x + 3) % 4, (x + 1) % 4, (x + 2) % 4
-        part = self.part
-        self.far_lo = self.lines.copy(part(far).at[LO], self.via.at[0], nxt)
-        self.far_hi = self.lines.copy(part(far).at[HI], self.via.at[1], prv)
+        me, nxt, prv = ring(self.axis)
+        left, right, far = (me + 3) % 4, (me + 1) % 4, (me + 2) % 4
+        self.far_lo = self.lines.copy(self.lo(far), self.via.at[0], nxt)
+        self.far_hi = self.lines.copy(self.hi(far), self.via.at[1], prv)
         self.rest = [
-            self.lines.copy(part(right).at[HI], self.got.at[2], nxt),
-            self.lines.copy(part(left).at[LO], self.got.at[0], prv),
+            self.lines.copy(self.hi(right), self.got.at[2], nxt),
+            self.lines.copy(self.lo(left), self.got.at[0], prv),
         ]
         for cp in (self.far_lo, self.far_hi, *self.rest):
             cp.start()
 
     def on(self):
-        x = coords()[3]
-        nxt, _, prv = x_peers()
-        left, right = (x + 3) % 4, (x + 1) % 4
+        me, nxt, prv = ring(self.axis)
+        left, right = (me + 3) % 4, (me + 1) % 4
         via = self.via
         self.far_lo.wait_recv()
-        via[0] = (via[0].astype(F32) + self.part(right)[LO].astype(F32)).astype(BF)
+        via[0] = (via[0].astype(F32) + self.lo(right)[...].astype(F32)).astype(BF)
         one = self.lines.copy(via.at[0], self.got.at[1], nxt)
         one.start()
         self.far_hi.wait_recv()
-        via[1] = (via[1].astype(F32) + self.part(left)[HI].astype(F32)).astype(BF)
+        via[1] = (via[1].astype(F32) + self.hi(left)[...].astype(F32)).astype(BF)
         two = self.lines.copy(via.at[1], self.got.at[3], prv)
         two.start()
         self.rest += [one, two]
@@ -147,11 +151,20 @@
         for cp in self.rest:
             cp.wait()
 
+    def others(self):
+        got = self.got
+        return got[0].astype(F32) + got[1].astype(F32), got[2].astype(F32) + got[3].astype(F32)
+
     def total(self, own):
-        got = self.got
-        lo = got[0].astype(F32) + got[1].astype(F32)
-        hi = got[2].astype(F32) + got[3].astype(F32)
-        return own + jnp.concatenate([lo, hi], axis=0)
+        return own + jnp.concatenate(self.others(), axis=0)
+
+
+def gather_x(lines, place):
+    return RingGather(lines, "x", lambda i: place(i, LO), lambda i: place(i, HI))
+
+
+def scatter_x(lines, parts, got, via):
+    return RingScatter(lines, "x", lambda i: parts.at[i, LO], lambda i: parts.at[i, HI], got, via)
 
 
 def one_hot_rows(rows, cols, expand):
@@ -286,12 +299,23 @@
         self.wait()
         y, zl, c, _, zh = coords()
         if self.z_first:
-            self._send(self._at(y, slice(None), c, pl.ds(0, 2 * self.rows)), y_peers())
+            rows = pl.ds(0, 2 * self.rows)
+            self.ring = RingGather(
+                self.lines, "y", lambda i: self._at(i, 0, c, rows), lambda i: self._at(i, 1, c, rows)
+            )
         else:
-            self._send(self._at(slice(None), zl, c, pl.ds(zh * self.rows, self.rows)), z_peers())
+            rows = lambda i: pl.ds(i // 2 * self.rows, self.rows)
+            self.ring = RingGather(
+                self.lines, "z", lambda i: self._at(pl.ds(0, 2), i % 2, c, rows(i)),
+                lambda i: self._at(pl.ds(2, 2), i % 2, c, rows(i)),
+            )
+        self.ring.start()
+
+    def on(self):
+        self.ring.on()
 
     def cores(self):
-        self.wait()
+        self.ring.finish()
         c = coords()[2]
         self._send(self._at(slice(None), slice(None), c, pl.ds(0, 2 * self.rows)), [core_peer()])
 
@@ -304,7 +328,7 @@
 class Scatter:
     def __init__(self, lines, part, bufs, rows, y_first, y_inner=False, columns=None):
         self.lines, self.part = lines, part
-        self.half, self.near_in, self.wide, self.wide_in = bufs
+        self.half, self.got, self.via, self.wide, self.wide_in = bufs
         self.rows, self.y_first, self.y_inner, self.pending = rows, y_first, y_inner, []
         self.columns = pl.ds(0, part.shape[-1]) if columns is None else columns
 
@@ -324,10 +348,15 @@
         place = (slice(None), 1 - c, slice(None)) if self.y_inner else (slice(None), slice(None), 1 - c)
         self._start([self.lines.copy(self.part.at[(*place, rows, self.columns)], self.half, core_peer())])
 
+    def _block(self, side, i):
+        if not self.y_first:
+            rows, pair = pl.ds(i // 2 * self.rows, self.rows), pl.ds(2 * side, 2)
+            return self.half.at[i % 2, pair, rows] if self.y_inner else self.half.at[pair, i % 2, rows]
+        return self.half.at[side, i] if self.y_inner else self.half.at[i, side]
+
     def first(self):
         self.wait()
-        y, zl, c, _, zh = coords()
-        z, rows, inner = zh * 2 + zl, self.rows, self.half.shape[1]
+        c, inner = coords()[2], self.half.shape[1]
 
         @pl.loop(0, 8)
         def _(i):
@@ -336,58 +365,64 @@
             both = self.part[(*place, slice(None), self.columns)].astype(F32) + self.half[a, b].astype(F32)
             self.half[a, b] = both.astype(BF)
 
+        self.ring = RingScatter(
+            self.lines, "y" if self.y_first else "z", lambda i: self._block(0, i), lambda i: self._block(1, i),
+            self.got, self.via,
+        )
+        self.ring.start()
+
+    def on(self):
+        self.ring.on()
+
+    def second(self):
+        self.ring.finish()
+        me = ring("y" if self.y_first else "z")[0]
+        for side, others in enumerate(self.ring.others()):
+            self.wide[side] = (self._block(side, me)[...].astype(F32) + others).astype(BF)
         copies = []
         for k in (1, 2, 3):
-            if self.y_first:
-                yy = (y + k) % 4
-                src, peer = self.half.at[:, yy] if self.y_inner else self.half.at[yy], y_peers()[k - 1]
-            else:
-                zz = (z + k) % 4
-                src, peer = self.half.at[:, zz % 2, pl.ds(zz // 2 * rows, rows)], z_peers()[k - 1]
-            copies.append(self.lines.copy(src, self.near_in.at[k - 1], peer))
+            peer = (z_peers if self.y_first else y_peers)()[k - 1]
+            copies.append(self.lines.copy(self._piece(k), self.wide_in.at[k - 1], peer))
         self._start(copies)
 
-    def second(self):
-        self.wait()
+    def _piece(self, k):
         y, zl, c, _, zh = coords()
-        z, rows = zh * 2 + zl, self.rows
-        copies = []
-        for i in range(self.wide.shape[0]):
-            if self.y_first:
-                total = (self.half[i, y] if self.y_inner else self.half[y, i]).astype(F32)
-            else:
-                total = self.half[i, zl, pl.ds(zh * rows, rows)].astype(F32)
-            for k in range(3):
-                total += self.near_in[k, i].astype(F32)
-            self.wide[i] = total.astype(BF)
-        for k in (1, 2, 3):
-            if self.y_first:
-                zz = (z + k) % 4
-                src, peer = self.wide.at[zz % 2, pl.ds(zz // 2 * rows, rows)], z_peers()[k - 1]
-            else:
-                src, peer = self.wide.at[(y + k) % 4], y_peers()[k - 1]
-            copies.append(self.lines.copy(src, self.wide_in.at[k - 1], peer))
-        self._start(copies)
+        if self.y_first:
+            zz = (zh * 2 + zl + k) % 4
+            return self.wide.at[zz % 2, pl.ds(zz // 2 * self.rows, self.rows)]
+        yy = (y + k) % 4
+        return self.wide.at[yy // 2, yy % 2]
 
     def total(self):
         self.wait()
-        y, zl, c, _, zh = coords()
-        if self.y_first:
-            total = self.wide[zl, pl.ds(zh * self.rows, self.rows)].astype(F32)
-        else:
-            total = self.wide[y].astype(F32)
+        total = self._piece(0)[...].astype(F32)
         for k in range(3):
             total += self.wide_in[k].astype(F32)
         return total
 
 
-def scatter_scratch(rows, n, y_first, y_inner=False):
-    half = pltpu.VMEM((2, 4, 2 * rows, n) if y_inner else (4, 2, 2 * rows, n), BF)
-    if y_first:
-        near_in, wide = pltpu.VMEM((3, 2, 2 * rows, n), BF), pltpu.VMEM((2, 2 * rows, n), BF)
-    else:
-        near_in, wide = pltpu.VMEM((3, 4, rows, n), BF), pltpu.VMEM((4, rows, n), BF)
-    return [half, near_in, wide, pltpu.VMEM((3, rows, n), BF)]
+class Both:
+    def __init__(self, lines, part, bufs, rows, split, width, y_inner=False):
+        n = len(bufs) // 2
+        self.parts = [
+            Scatter(lines, part, bufs[:n], rows, False, y_inner, pl.ds(0, split)),
+            Scatter(lines, part, bufs[n:], rows, True, y_inner, pl.ds(split, width - split)),
+        ]
+
+    def __getattr__(self, step):
+        return lambda: [getattr(p, step)() for p in self.parts]
+
+    def sums(self):
+        return jnp.concatenate([p.total().astype(BF) for p in self.parts], axis=1)
+
+
+def scatter_scratch(rows, split, width, y_inner=False):
+    found = []
+    for n, y_first in ((split, False), (width - split, True)):
+        half = (2, 4, 2 * rows, n) if y_inner else (4, 2, 2 * rows, n)
+        block = (2 * rows, n) if y_first else (2, rows, n)
+        found += [pltpu.VMEM(s, BF) for s in (half, (4, *block), (2, *block), (2, *block), (3, rows, n))]
+    return found
 
 
 def dot(a, b):
@@ -445,8 +480,7 @@
     "normed", "q_ref", "k_ref", "v_ref", "p0", "p1", "p2", "p3",
     "att", "att_grad", "middle", "wo", "ntwo", "up_grad", "hidden", "pre_grad", "branch", "part_a", "part_c",
     "got_a", "via_a", "got_b", "via_b", "got_c", "via_c", "swap_out", "swap_in", "dk_t", "dv_t",
-    "sq0", "sq1", "sq2", "sq3", "sr0", "sr1", "sr2", "sr3", "su0", "su1", "su2", "su3",
-    "sd0", "sd1", "sd2", "sd3", "so0", "so1", "so2", "so3", "fin_o", "fin_d", "send", "recv",
+    *(f"s{w}{k}" for w in "qudo" for k in range(10)), "fin_o", "fin_d", "send", "recv",
 )
 
 
@@ -463,10 +497,10 @@
     shapes += [block] * 7
     shapes += [got, via] * 3 + [V((128, D), BF), V((128, D), BF)]
     shapes += [V((128, GROUP), F32), V((128, GROUP), F32)]
-    shapes += scatter_scratch(48, 640, False) + scatter_scratch(48, 512, True) + scatter_scratch(48, D, False)
-    shapes += scatter_scratch(48, D, True, True) + scatter_scratch(16, D, True, True)
+    shapes += scatter_scratch(48, 640, 1152) + scatter_scratch(48, 768, D)
+    shapes += scatter_scratch(48, 768, D, True) + scatter_scratch(16, 768, D, True)
     shapes += [V((16, D), BF), V((48, D), BF)]
-    shapes += [pltpu.SemaphoreType.DMA((160,)), pltpu.SemaphoreType.DMA((160,))]
+    shapes += [pltpu.SemaphoreType.DMA((300,)), pltpu.SemaphoreType.DMA((300,))]
     assert len(shapes) == len(NAMES)
     return shapes
 
@@ -511,6 +545,7 @@
     g = Refs()
     for name, ref in zip(NAMES, scratch):
         setattr(g, name, ref)
+    bufs = lambda w: [getattr(g, f"s{w}{k}") for k in range(10)]
     y, zl, c, x, zh = coords()
     lines = Lines(g.send, g.recv)
     scale = HEAD_DIM**-0.5
@@ -527,28 +562,16 @@
     g.src_o[...] = sixteen(out_w[...].astype(F32))
     pl.semaphore_wait(pltpu.get_barrier_semaphore(), greetings)
 
-    ring_one = RingGather(lines, lambda i: g.normed.at[i, zh])
-    ring_two = RingGather(lines, lambda i: g.normed.at[i, 1 - zh])
+    ring_one = gather_x(lines, lambda i, h: g.normed.at[i, zh, h])
+    ring_two = gather_x(lines, lambda i, h: g.normed.at[i, 1 - zh, h])
     swap = lines.copy(g.normed.at[x, zh], g.normed.at[x, zh], zh_peer())
     plan_q = spread(lines, g.src_q, g.got_q)
     start_all(plan_q, g.src_q, g.got_q)
+    swap_o = lines.copy(g.src_o, g.full_o.at[zl, c, x, pl.ds(zh * 16, 16)], swap_xy())
+    swap_d = lines.copy(down, g.full_d.at[zl, c, x, pl.ds(zh * 48, 48)], swap_xy())
     ring_one.start()
     swap.start()
-    plan_u = spread(lines, g.src_u, g.got_u)
-    start_all(plan_u, g.src_u, g.got_u)
-    swap_o = lines.copy(g.src_o, g.full_o.at[zl, c, x, pl.ds(zh * 16, 16)], swap_xy())
-    swap_d = lines.copy(down, g.full_d.at[zl, c, x, pl.ds(zh * 48, 48)], swap_xy())
-
-    @pl.when(x != y)
-    def _():
-        swap_o.start()
-        swap_d.start()
-
-    @pl.when(x == y)
-    def _():
-        g.full_o[zl, c, x, pl.ds(zh * 16, 16)] = g.src_o[...]
-        g.full_d[zl, c, x, pl.ds(zh * 48, 48)] = down[...]
-
+    pl.when(x != y)(swap_o.start)
     rows = one_hot_rows(48, 64, False)
     wait_all(plan_q)
     g.full_q[y, zl, c, pl.ds(zh * 48, 48)] = pick(rows, g.got_q[...].reshape(64, 1152))
@@ -556,32 +579,37 @@
         Gather(lines, g.full_q, 48, True, False, pl.ds(0, 640)),
         Gather(lines, g.full_q, 48, False, False, pl.ds(640, 512)),
     ]
-    for t in gather_q:
-        t.near()
-    ring_one.on()
-    for t in gather_q:
-        t.wide()
     gather_o = Gather(lines, g.full_o, 16, False, True)
     gather_u = Gather(lines, g.full_u, 48, True)
     gather_d = Gather(lines, g.full_d, 48, False, True)
-
-    @pl.when(x != y)
+    for t in gather_q:
+        t.near()
+
+    @pl.when(x == y)
     def _():
-        swap_o.wait()
-        swap_d.wait()
-
+        g.full_o[zl, c, x, pl.ds(zh * 16, 16)] = g.src_o[...]
+        g.full_d[zl, c, x, pl.ds(zh * 48, 48)] = down[...]
+
+    ring_one.on()
+    pl.when(x != y)(swap_o.wait)
     gather_o.near()
     swap.wait_recv()
     ring_two.start()
+    plan_u = spread(lines, g.src_u, g.got_u)
+    start_all(plan_u, g.src_u, g.got_u)
+    pl.when(x != y)(swap_d.start)
+    for t in (*gather_q, gather_o):
+        t.wide()
+    for t in (*gather_q, gather_o):
+        t.on()
+    ring_two.on()
+    for t in gather_q:
+        t.cores()
     wait_all(plan_u)
     g.full_u[y, zl, c, pl.ds(zh * 48, 48)] = pick(rows, g.got_u[...].reshape(64, D))
-    gather_d.near()
     gather_u.near()
+    gather_o.cores()
     ring_one.finish()
-    for t in gather_q:
-        t.cores()
-    gather_o.wide()
-    ring_two.on()
     for t in gather_q:
         t.wait()
 
@@ -603,14 +631,15 @@
                     g.v_ref[h, :, zz] = head
 
     project(zh, True)
+    pl.when(x != y)(swap_d.wait)
+    gather_d.near()
     ring_two.finish()
     swap.wait_send()
-    ring_up = RingGather(lines, lambda i: g.up_grad.at[i])
+    ring_up = gather_x(lines, lambda i, h: g.up_grad.at[i, h])
     ring_up.start()
+    project(1 - zh, False)
+    gather_u.wide()
     gather_d.wide()
-    gather_u.wide()
-    project(1 - zh, False)
-    gather_o.cores()
 
     probs = [g.p0, g.p1, g.p2, g.p3]
 
@@ -645,14 +674,16 @@
             parts[:, :, cols(t, n)] = made.astype(BF).reshape(4, 128, n)
 
     to_parts(g.part_a, g.att[...].reshape(512, RANK_COLS), lambda t: g.wo[:, cols(t, 512)], False, 3)
-    ring_a = RingScatter(lines, lambda i: g.part_a.at[i], g.got_a, g.via_a)
+    ring_a = scatter_x(lines, g.part_a, g.got_a, g.via_a)
     ring_a.start()
+    gather_u.on()
+    gather_d.on()
     ring_up.finish()
     ring_a.on()
     ring_a.finish()
     g.middle[...] = ring_a.total(tokens[...].astype(F32) + g.part_a[x].astype(F32))
     g.ntwo[x] = normalize(g.middle[...])[1].astype(BF)
-    ring_n = RingGather(lines, lambda i: g.ntwo.at[i])
+    ring_n = gather_x(lines, lambda i, h: g.ntwo.at[i, h])
     ring_n.start()
     gather_d.cores()
     gather_u.cores()
@@ -690,7 +721,7 @@
 
     pre_all = g.pre_grad[...].reshape(512, D)
     to_parts(g.part_a, pre_all, lambda t: full_rows(g.full_u, t), True, 2)
-    ring_b = RingScatter(lines, lambda i: g.part_a.at[i], g.got_b, g.via_b)
+    ring_b = scatter_x(lines, g.part_a, g.got_b, g.via_b)
     ring_b.start()
 
     def weight_grad(full, left_of, right):
@@ -703,28 +734,34 @@
                 full[t // 2, t % 2] = made.reshape(full.shape[2:])
 
     weight_grad(g.full_u, lambda t: g.ntwo[:, :, cols(t, 384)].reshape(512, 384), pre_all)
-    scatter_u = Scatter(lines, g.full_u, (g.su0, g.su1, g.su2, g.su3), 48, False)
+    scatter_u = Both(lines, g.full_u, bufs("u"), 48, 768, D)
     scatter_u.cores()
     ring_b.on()
     to_parts(g.part_c, g.hidden[...].reshape(512, D), lambda t: full_cols(g.full_d, t, 512), False, 3)
     scatter_u.first()
     weight_grad(g.full_d, lambda t: g.hidden[:, :, cols(t, 384)].reshape(512, 384), up_all)
-    scatter_d = Scatter(lines, g.full_d, (g.sd0, g.sd1, g.sd2, g.sd3), 48, True, True)
+    scatter_d = Both(lines, g.full_d, bufs("d"), 48, 768, D, True)
     scatter_d.cores()
     ring_b.finish()
 
     grad_input[...] = grad_in[...].astype(F32) + rms_back(ring_b.total(g.part_a[x].astype(F32)), g.middle[...])
     g.branch[x] = grad_input[...].astype(BF)
-    ring_g = RingGather(lines, lambda i: g.branch.at[i])
+    ring_g = gather_x(lines, lambda i, h: g.branch.at[i, h])
     ring_g.start()
+    scatter_u.on()
+    ring_g.on()
     scatter_d.first()
-    ring_g.on()
     ring_g.finish()
-    ring_c = RingScatter(lines, lambda i: g.part_c.at[i], g.got_c, g.via_c)
+    ring_c = scatter_x(lines, g.part_c, g.got_c, g.via_c)
     ring_c.start()
 
     branch_all = g.branch[...].reshape(512, D)
+    scatter_u.second()
     g.att_grad[...] = dot_nt(branch_all, g.wo[...]).astype(BF).reshape(4, 128, RANK_COLS)
+    d_out = dot_tn(g.att[...].reshape(512, RANK_COLS), branch_all).astype(BF)
+    g.full_o[...] = pick(one_hot_rows(512, RANK_COLS, True), d_out).reshape(2, 2, 4, 32, D)
+    scatter_o = Both(lines, g.full_o, bufs("o"), 16, 768, D, True)
+    scatter_o.cores()
 
     @pl.loop(0, RANK_HEADS)
     def _(h):
@@ -750,6 +787,8 @@
         g.v_ref[h] = g.dv_t[...].T.astype(BF).reshape(4, 2, 128, 128)
 
     ring_c.on()
+    scatter_d.on()
+    scatter_o.first()
 
     def side(ref, zz):
         return [ref[h, :, zz].reshape(512, 128) for h in range(RANK_HEADS)]
@@ -763,13 +802,10 @@
         to_parts(parts, left, lambda t: g.full_q[pl.ds(t * 2, 2), :, :, :, 1152 - n :].reshape(768, n), True, 2)
 
     first_parts(g.part_a, 1 - zh, False)
-    ring_e = RingScatter(lines, lambda i: g.part_a.at[i], g.got_a, g.via_a)
+    ring_e = scatter_x(lines, g.part_a, g.got_a, g.via_a)
     ring_e.start()
-    scatter_u.second()
-    ring_c.finish()
-    block_out[...] = ring_c.total(g.middle[...] + g.part_c[x].astype(F32)).astype(BF)
-    first_parts(g.part_c, zh, True)
-    ring_f = RingScatter(lines, lambda i: g.part_c.at[i], g.got_b, g.via_b)
+    first_parts(g.ntwo, zh, True)
+    ring_f = scatter_x(lines, g.ntwo, g.got_b, g.via_b)
     ring_f.start()
 
     dq_all = jnp.concatenate([g.q_ref[h].reshape(512, 128) for h in range(RANK_HEADS)], axis=1)
@@ -781,51 +817,43 @@
     def _(t):
         mine = g.normed[:, zh, :, cols(t, 384)].reshape(512, 384)
         every = g.normed[:, :, :, cols(t, 384)].reshape(GROUP, 384)
-        g.full_q[t, :, :, :, :RANK_COLS] = dot_tn(mine, dq_all).astype(BF).reshape(2, 2, 96, RANK_COLS)
-        g.full_q[t, :, :, :, RANK_COLS:] = dot_tn(every, dkv_all).astype(BF).reshape(2, 2, 96, 768)
-
-    scatter_q = [
-        Scatter(lines, g.full_q, (g.sq0, g.sq1, g.sq2, g.sq3), 48, False, False, pl.ds(0, 640)),
-        Scatter(lines, g.full_q, (g.sr0, g.sr1, g.sr2, g.sr3), 48, True, False, pl.ds(640, 512)),
-    ]
-    for t in scatter_q:
-        t.cores()
+        g.full_u[t, :, :, :, :RANK_COLS] = dot_tn(mine, dq_all).astype(BF).reshape(2, 2, 96, RANK_COLS)
+        g.full_u[t, :, :, :, RANK_COLS:1152] = dot_tn(every, dkv_all).astype(BF).reshape(2, 2, 96, 768)
+
+    scatter_q = Both(lines, g.full_u, bufs("q"), 48, 640, 1152)
+    scatter_q.cores()
     ring_e.on()
     scatter_d.second()
-    d_out = dot_tn(g.att[...].reshape(512, RANK_COLS), branch_all).astype(BF)
-    g.full_o[...] = pick(one_hot_rows(512, RANK_COLS, True), d_out).reshape(2, 2, 4, 32, D)
-    scatter_o = Scatter(lines, g.full_o, (g.so0, g.so1, g.so2, g.so3), 16, True, True)
-    scatter_o.cores()
-    for t in scatter_q:
-        t.first()
+    scatter_q.first()
+    scatter_o.on()
+    ring_c.finish()
+    block_out[...] = ring_c.total(g.middle[...] + g.part_c[x].astype(F32)).astype(BF)
+    spread_rows = one_hot_rows(64, 48, True)
+    g.got_u[...] = pick(spread_rows, scatter_u.sums()).reshape(4, 16, D)
+    plan_u = gather_home(lines, g.got_u, out_u)
+    start_all(plan_u, g.got_u, out_u)
     ring_f.on()
-    scatter_o.first()
+    scatter_q.on()
+    scatter_o.second()
     ring_e.finish()
     g.swap_out[...] = ring_e.total(g.part_a[x].astype(F32)).astype(BF)
     back = lines.copy(g.swap_out, g.swap_in, zh_peer())
     back.start()
-
-    spread_rows = one_hot_rows(64, 48, True)
-    g.got_u[...] = pick(spread_rows, scatter_u.total().astype(BF)).reshape(4, 16, D)
-    plan_u = gather_home(lines, g.got_u, out_u)
-    start_all(plan_u, g.got_u, out_u)
-    for t in scatter_q:
-        t.second()
-    scatter_o.second()
-    g.fin_d[...] = scatter_d.total().astype(BF)
+    scatter_q.second()
+    g.fin_d[...] = scatter_d.sums()
     home_d = lines.copy(g.fin_d, out_d, swap_xy())
     home_o = lines.copy(g.fin_o, out_o, swap_xy())
     pl.when(x != y)(home_d.start)
+    g.fin_o[...] = scatter_o.sums()
+    pl.when(x != y)(home_o.start)
+
+    g.got_q[...] = pick(spread_rows, scatter_q.sums()).reshape(4, 16, 1152)
+    plan_q = gather_home(lines, g.got_q, out_q)
+    start_all(plan_q, g.got_q, out_q)
     ring_f.finish()
     back.wait()
-    h_one = ring_f.total(g.part_c[x].astype(F32)) + g.swap_in[...].astype(F32)
+    h_one = ring_f.total(g.ntwo[x].astype(F32)) + g.swap_in[...].astype(F32)
     grad_input[...] += rms_back(h_one, tokens[...].astype(F32))
-    both = jnp.concatenate([scatter_q[0].total().astype(BF), scatter_q[1].total().astype(BF)], axis=1)
-    g.got_q[...] = pick(spread_rows, both).reshape(4, 16, 1152)
-    plan_q = gather_home(lines, g.got_q, out_q)
-    start_all(plan_q, g.got_q, out_q)
-    g.fin_o[...] = scatter_o.total().astype(BF)
-    pl.when(x != y)(home_o.start)
 
     @pl.when(x == y)
     def _():

time: 215 us -> 199 us (0.926)
  Pallas kernels: 213 us -> 196 us
    pallas_call x1, Pallas kernels: 210 us -> 193 us  [per_device(): pl.pallas_call(layer_kernel, out_shape=shapes_of(outs), in_specs=[smem] *...]
where the time goes in v1:
time: 199 us; the launch traced here: 196 us
  Pallas kernels  196 us (98%)
    pallas_call x1, Pallas kernels, per_device(): pl.pallas_call(layer_kernel, out_shape=shapes_of(outs), in_specs=[smem] *...  193 us

profile of v1, /device:TPU:0, one launch (start us, length us, event | category | flops | bytes accessed | tf_op | source)
XLA Modules:
  0.0 196.3 jit_solution(15560878008539930175)
XLA Ops:
  0.6 192.5 %layer_kernel.1 = (bf16[128,1536]{1,0:T(8,128)(2,1)}, f32[128,1536]{1,0:T(8,128)}, bf16[4,16,1152]{2,1,0:T(8,128)(2,1)}, bf16[4,16,1536]{2,1,0:T(8,128)(2,1)}, b...) custom-call(s32[1,6]{1,0:T(1,128)} %lengths.1, s32[1,6]{1,0:T(1,128)} %levels.1, bf16[128,1536]{1,0:T(8,128)(2,1)} %bitcast.8, ...), custom_call_target="tpu_custom_call" | custom-call | tf_op jit(solution)/shard_map/layer_kernel/pallas_call | solution.py:913
  193.2 3.1 %finish_kernel.1 = (bf16[128,1536]{1,0:T(8,128)(2,1)}, f32[128,1536]{1,0:T(8,128)}, f32[1,12]{1,0:T(1,128)}, f32[12,4608]{1,0:T(8,128)}, f32[12,1536]{1,0:T(8,12...) custom-call(bf16[128,1536]{1,0:T(8,128)(2,1)} %get-tuple-element.22.block, ...), custom_call_target="tpu_custom_call" | custom-call | tf_op jit(solution)/shard_map/finish_kernel/pallas_call | solution.py:927

commit v2 on v1

--- a/solution.py
+++ b/solution.py
@@ -108,6 +108,11 @@
         two.start()
         self.rest += [one, two]
 
+    def near(self):
+        for cp in self.rest[:2]:
+            cp.wait()
+        self.rest = self.rest[2:]
+
     def finish(self):
         self.first.wait_send()
         self.second.wait_send()
@@ -120,15 +125,25 @@
         self.lines, self.axis, self.lo, self.hi, self.got, self.via = lines, axis, lo, hi, got, via
 
     def start(self):
+        self.start_far()
+        self.start_near()
+
+    def start_far(self):
         me, nxt, prv = ring(self.axis)
-        left, right, far = (me + 3) % 4, (me + 1) % 4, (me + 2) % 4
+        far = (me + 2) % 4
         self.far_lo = self.lines.copy(self.lo(far), self.via.at[0], nxt)
         self.far_hi = self.lines.copy(self.hi(far), self.via.at[1], prv)
+        self.far_lo.start()
+        self.far_hi.start()
+
+    def start_near(self):
+        me, nxt, prv = ring(self.axis)
+        left, right = (me + 3) % 4, (me + 1) % 4
         self.rest = [
             self.lines.copy(self.hi(right), self.got.at[2], nxt),
             self.lines.copy(self.lo(left), self.got.at[0], prv),
         ]
-        for cp in (self.far_lo, self.far_hi, *self.rest):
+        for cp in self.rest:
             cp.start()
 
     def on(self):
@@ -401,19 +416,30 @@
         return total
 
 
-class Both:
-    def __init__(self, lines, part, bufs, rows, split, width, y_inner=False):
-        n = len(bufs) // 2
-        self.parts = [
-            Scatter(lines, part, bufs[:n], rows, False, y_inner, pl.ds(0, split)),
-            Scatter(lines, part, bufs[n:], rows, True, y_inner, pl.ds(split, width - split)),
-        ]
+class Pair:
+    def __init__(self, *parts):
+        self.parts = parts
 
     def __getattr__(self, step):
         return lambda: [getattr(p, step)() for p in self.parts]
 
     def sums(self):
         return jnp.concatenate([p.total().astype(BF) for p in self.parts], axis=1)
+
+
+def gather_both(lines, full, rows, split, width, y_inner=False):
+    return Pair(
+        Gather(lines, full, rows, True, y_inner, pl.ds(0, split)),
+        Gather(lines, full, rows, False, y_inner, pl.ds(split, width - split)),
+    )
+
+
+def scatter_both(lines, part, bufs, rows, split, width, y_inner=False):
+    n = len(bufs) // 2
+    return Pair(
+        Scatter(lines, part, bufs[:n], rows, False, y_inner, pl.ds(0, split)),
+        Scatter(lines, part, bufs[n:], rows, True, y_inner, pl.ds(split, width - split)),
+    )
 
 
 def scatter_scratch(rows, split, width, y_inner=False):
@@ -478,9 +504,10 @@
 NAMES = (
     "full_q", "full_u", "full_d", "full_o", "got_q", "got_u", "src_q", "src_u", "src_o",
     "normed", "q_ref", "k_ref", "v_ref", "p0", "p1", "p2", "p3",
-    "att", "att_grad", "middle", "wo", "ntwo", "up_grad", "hidden", "pre_grad", "branch", "part_a", "part_c",
-    "got_a", "via_a", "got_b", "via_b", "got_c", "via_c", "swap_out", "swap_in", "dk_t", "dv_t",
-    *(f"s{w}{k}" for w in "qudo" for k in range(10)), "fin_o", "fin_d", "send", "recv",
+    "att", "att_grad", "middle", "wo", "ntwo", "up_grad", "hidden", "pre_grad", "branch", "part_a",
+    "got_a", "via_a", "got_b", "via_b", "swap_in", "dk_t", "dv_t",
+    *(f"s{w}{k}" for w in "qudo" for k in range(10)), "send", "recv",
+    "tokens", "qkv", "grad_in", "up", "out_w", "down", "angles", "load",
 )
 
 
@@ -494,13 +521,15 @@
     shapes += [V((4, 2, 128, D), BF), V((3, 4, 128, 128), BF), kv, kv]
     shapes += [V((3, 128, 256 * (i + 1)), BF) for i in range(4)]
     shapes += [V((4, 128, RANK_COLS), BF), V((4, 128, RANK_COLS), BF), V((128, D), F32), V((RANK_COLS, D), BF)]
-    shapes += [block] * 7
-    shapes += [got, via] * 3 + [V((128, D), BF), V((128, D), BF)]
+    shapes += [block] * 6
+    shapes += [got, via] * 2 + [V((128, D), BF)]
     shapes += [V((128, GROUP), F32), V((128, GROUP), F32)]
-    shapes += scatter_scratch(48, 640, 1152) + scatter_scratch(48, 768, D)
+    shapes += scatter_scratch(48, RANK_COLS, 1152) + scatter_scratch(48, 768, D)
     shapes += scatter_scratch(48, 768, D, True) + scatter_scratch(16, 768, D, True)
-    shapes += [V((16, D), BF), V((48, D), BF)]
     shapes += [pltpu.SemaphoreType.DMA((300,)), pltpu.SemaphoreType.DMA((300,))]
+    rows = V((128, D), BF)
+    shapes += [rows, V((12, 3 * D), BF), rows, V((12, FF), BF), V((12, D), BF), V((48, D), BF)]
+    shapes += [V((4, 2, 128, 128), F32), pltpu.SemaphoreType.DMA((7,))]
     assert len(shapes) == len(NAMES)
     return shapes
 
@@ -539,7 +568,7 @@
 
 
 def layer_kernel(
-    lengths, levels, tokens, grad_in, qkv, out_w, up, down, gain_one, gain_two, angles,
+    lengths, levels, gain_one, gain_two, tokens_in, grad_in_in, qkv_in, out_w_in, up_in, down_in, angles_in,
     block_out, grad_input, out_q, out_u, out_d, out_o, *scratch
 ):
     g = Refs()
@@ -551,15 +580,30 @@
     scale = HEAD_DIM**-0.5
     greetings = greet()
 
+    tokens, grad_in, qkv, out_w, up, down, angles = g.tokens, g.grad_in, g.qkv, g.out_w, g.up, g.down, g.angles
+    pairs = [
+        (tokens_in, tokens), (qkv_in, qkv), (grad_in_in, grad_in), (up_in, up), (out_w_in, out_w), (down_in, down),
+        (angles_in, angles),
+    ]
+    loads = [pltpu.make_async_copy(a, b, g.load.at[k]) for k, (a, b) in enumerate(pairs)]
+    for cp in loads:
+        cp.start()
+    loads[0].wait()
     g.normed[x, zh] = normalize(tokens[...].astype(F32))[1].astype(BF)
-    g.up_grad[x] = grad_in[...]
     one, two = column(gain_one[...].astype(F32)), column(gain_two[...].astype(F32))
+    loads[1].wait()
     for i in range(4):
         for j in range(3):
             at = j * D + i * RANK_COLS
             g.src_q[i, :, j * RANK_COLS : (j + 1) * RANK_COLS] = sixteen(qkv[:, at : at + RANK_COLS].astype(F32) * one)
+    for cp in loads[2:5]:
+        cp.wait()
+    g.up_grad[x] = grad_in[...]
+    for i in range(4):
         g.src_u[i] = sixteen(up[:, i * D : (i + 1) * D].astype(F32) * two)
     g.src_o[...] = sixteen(out_w[...].astype(F32))
+    for cp in loads[5:]:
+        cp.wait()
     pl.semaphore_wait(pltpu.get_barrier_semaphore(), greetings)
 
     ring_one = gather_x(lines, lambda i, h: g.normed.at[i, zh, h])
@@ -569,21 +613,17 @@
     start_all(plan_q, g.src_q, g.got_q)
     swap_o = lines.copy(g.src_o, g.full_o.at[zl, c, x, pl.ds(zh * 16, 16)], swap_xy())
     swap_d = lines.copy(down, g.full_d.at[zl, c, x, pl.ds(zh * 48, 48)], swap_xy())
+    swap.start()
     ring_one.start()
-    swap.start()
     pl.when(x != y)(swap_o.start)
     rows = one_hot_rows(48, 64, False)
     wait_all(plan_q)
     g.full_q[y, zl, c, pl.ds(zh * 48, 48)] = pick(rows, g.got_q[...].reshape(64, 1152))
-    gather_q = [
-        Gather(lines, g.full_q, 48, True, False, pl.ds(0, 640)),
-        Gather(lines, g.full_q, 48, False, False, pl.ds(640, 512)),
-    ]
-    gather_o = Gather(lines, g.full_o, 16, False, True)
-    gather_u = Gather(lines, g.full_u, 48, True)
-    gather_d = Gather(lines, g.full_d, 48, False, True)
-    for t in gather_q:
-        t.near()
+    gather_q = gather_both(lines, g.full_q, 48, 256, 1152)
+    gather_o = Gather(lines, g.full_o, 16, True, True)
+    gather_u = gather_both(lines, g.full_u, 48, 768, D)
+    gather_d = gather_both(lines, g.full_d, 48, 768, D, True)
+    gather_q.near()
 
     @pl.when(x == y)
     def _():
@@ -591,27 +631,22 @@
         g.full_d[zl, c, x, pl.ds(zh * 48, 48)] = down[...]
 
     ring_one.on()
+    gather_q.wide()
+    pl.when(x != y)(swap_d.start)
+    swap.wait_recv()
+    ring_two.start()
+    gather_q.on()
     pl.when(x != y)(swap_o.wait)
     gather_o.near()
-    swap.wait_recv()
-    ring_two.start()
     plan_u = spread(lines, g.src_u, g.got_u)
     start_all(plan_u, g.src_u, g.got_u)
-    pl.when(x != y)(swap_d.start)
-    for t in (*gather_q, gather_o):
-        t.wide()
-    for t in (*gather_q, gather_o):
-        t.on()
     ring_two.on()
-    for t in gather_q:
-        t.cores()
-    wait_all(plan_u)
-    g.full_u[y, zl, c, pl.ds(zh * 48, 48)] = pick(rows, g.got_u[...].reshape(64, D))
-    gather_u.near()
-    gather_o.cores()
+    gather_q.cores()
+    gather_o.wide()
+    pl.when(x != y)(swap_d.wait)
+    gather_d.near()
     ring_one.finish()
-    for t in gather_q:
-        t.wait()
+    gather_q.wait()
 
     def project(zz, own_half):
         block = g.normed[:, zz].reshape(512, D)
@@ -631,20 +666,21 @@
                     g.v_ref[h, :, zz] = head
 
     project(zh, True)
-    pl.when(x != y)(swap_d.wait)
-    gather_d.near()
+    gather_o.on()
+    gather_d.wide()
+    wait_all(plan_u)
+    g.full_u[y, zl, c, pl.ds(zh * 48, 48)] = pick(rows, g.got_u[...].reshape(64, D))
+    gather_u.near()
     ring_two.finish()
     swap.wait_send()
     ring_up = gather_x(lines, lambda i, h: g.up_grad.at[i, h])
     ring_up.start()
     project(1 - zh, False)
-    gather_u.wide()
-    gather_d.wide()
+    gather_o.cores()
 
     probs = [g.p0, g.p1, g.p2, g.p3]
 
-    @pl.loop(0, RANK_HEADS)
-    def _(h):
+    def attend(h):
         for i in range(4):
             n = 256 * (i + 1)
             keys = g.k_ref[h, : i + 1].reshape(n, 128)
@@ -660,7 +696,10 @@
             probs[i][h] = p
             g.att[i, :, pl.ds(pl.multiple_of(h * 128, 128), 128)] = dot(p, values).astype(BF)
 
+    attend(0)
+    gather_d.on()
     ring_up.on()
+    pl.loop(1, RANK_HEADS)(attend)
     gather_o.wait()
     g.wo[...] = pick(one_hot_rows(RANK_COLS, 512, False), g.full_o[...].reshape(512, D))
 
@@ -670,24 +709,27 @@
         @pl.loop(0, tiles)
         def _(t):
             right = right_of(t)
-            made = dot_nt(left, right) if transposed else dot(left, right)
+            made = dot_nt(left(), right) if transposed else dot(left(), right)
             parts[:, :, cols(t, n)] = made.astype(BF).reshape(4, 128, n)
 
-    to_parts(g.part_a, g.att[...].reshape(512, RANK_COLS), lambda t: g.wo[:, cols(t, 512)], False, 3)
+    to_parts(g.part_a, lambda: g.att[...].reshape(512, RANK_COLS), lambda t: g.wo[:, cols(t, 512)], False, 3)
     ring_a = scatter_x(lines, g.part_a, g.got_a, g.via_a)
     ring_a.start()
+    gather_u.wide()
+    gather_d.cores()
+
     gather_u.on()
-    gather_d.on()
     ring_up.finish()
+    gather_d.wait()
     ring_a.on()
+    up_all = lambda: g.up_grad[...].reshape(512, D)
+    to_parts(g.pre_grad, up_all, lambda t: g.full_d[t].reshape(768, D), True, 2)
+    gather_u.cores()
     ring_a.finish()
     g.middle[...] = ring_a.total(tokens[...].astype(F32) + g.part_a[x].astype(F32))
     g.ntwo[x] = normalize(g.middle[...])[1].astype(BF)
     ring_n = gather_x(lines, lambda i, h: g.ntwo.at[i, h])
     ring_n.start()
-    gather_d.cores()
-    gather_u.cores()
-    ring_n.on()
 
     def full_rows(ref, t):
         return ref[pl.ds(t * 2, 2)].reshape(768, ref.shape[-1])
@@ -695,76 +737,84 @@
     def full_cols(ref, t, n):
         return ref[:, :, :, :, cols(t, n)].reshape(D, n)
 
-    gather_d.wait()
-    up_all = g.up_grad[...].reshape(512, D)
-    to_parts(g.pre_grad, up_all, lambda t: g.full_d[t].reshape(768, D), True, 2)
     gather_u.wait()
+
+    def feed_forward(blocks, tile):
+        rows = 128 * len(blocks)
+        at = [(2 * i + zh) * 128 + lax.broadcasted_iota(jnp.int32, (128, 1), 0) for i in blocks]
+        width = jnp.concatenate([documents(lengths, levels, p)[1] for p in at], axis=0)
+
+        @pl.loop(0, D // tile)
+        def _(t):
+            normed_rows = jnp.concatenate([g.ntwo[i] for i in blocks], axis=0)
+            pre = dot(normed_rows, full_cols(g.full_u, t, tile))
+            unit = x * D + t * tile + lax.broadcasted_iota(jnp.int32, (rows, tile), 1)
+            mask = unit < width
+            act, slope = gelu_both(pre)
+            act = jnp.where(mask, act, 0.0).astype(BF)
+            slope = jnp.where(mask, slope, 0.0)
+            for k, i in enumerate(blocks):
+                own = slice(128 * k, 128 * (k + 1))
+                g.hidden[i, :, cols(t, tile)] = act[own]
+                back = g.pre_grad[i, :, cols(t, tile)].astype(F32)
+                g.pre_grad[i, :, cols(t, tile)] = (slope[own] * back).astype(BF)
+
+        @pl.loop(0, 2)
+        def _(t):
+            pre_rows = jnp.concatenate([g.pre_grad[i] for i in blocks], axis=0)
+            made = dot_nt(pre_rows, full_rows(g.full_u, t)).astype(BF)
+            for k, i in enumerate(blocks):
+                g.part_a[i, :, cols(t, 768)] = made[128 * k : 128 * (k + 1)]
+
+    feed_forward([x], 512)
+    ring_n.on()
+    ring_n.near()
+    ring_b = scatter_x(lines, g.part_a, g.got_b, g.via_b)
+    feed_forward([(x + 3) % 4, (x + 1) % 4], 256)
+    ring_b.start_near()
     ring_n.finish()
-
-    width = jnp.concatenate(
-        [
-            documents(lengths, levels, (2 * i + zh) * 128 + lax.broadcasted_iota(jnp.int32, (128, 1), 0))[1]
-            for i in range(4)
-        ],
-        axis=0,
-    )
-
-    @pl.loop(0, 6)
-    def _(t):
-        pre = dot(g.ntwo[...].reshape(512, D), full_cols(g.full_u, t, 256))
-        unit = x * D + t * 256 + lax.broadcasted_iota(jnp.int32, (512, 256), 1)
-        mask = unit < width
-        act, slope = gelu_both(pre)
-        g.hidden[:, :, cols(t, 256)] = jnp.where(mask, act, 0.0).astype(BF).reshape(4, 128, 256)
-        back = g.pre_grad[:, :, cols(t, 256)].reshape(512, 256).astype(F32)
-        g.pre_grad[:, :, cols(t, 256)] = jnp.where(mask, slope * back, 0.0).astype(BF).reshape(4, 128, 256)
-
-    pre_all = g.pre_grad[...].reshape(512, D)
-    to_parts(g.part_a, pre_all, lambda t: full_rows(g.full_u, t), True, 2)
-    ring_b = scatter_x(lines, g.part_a, g.got_b, g.via_b)
-    ring_b.start()
+    feed_forward([(x + 2) % 4], 512)
+    ring_b.start_far()
+    pre_all = lambda: g.pre_grad[...].reshape(512, D)
 
     def weight_grad(full, left_of, right):
         @pl.loop(0, 4)
         def _(t):
-            made = dot_tn(left_of(t), right).astype(BF)
+            made = dot_tn(left_of(t), right()).astype(BF)
             if full.shape[0] == 4:
                 full[t] = made.reshape(full.shape[1:])
             else:
                 full[t // 2, t % 2] = made.reshape(full.shape[2:])
 
     weight_grad(g.full_u, lambda t: g.ntwo[:, :, cols(t, 384)].reshape(512, 384), pre_all)
-    scatter_u = Both(lines, g.full_u, bufs("u"), 48, 768, D)
+    scatter_u = scatter_both(lines, g.full_u, bufs("u"), 48, 768, D)
     scatter_u.cores()
     ring_b.on()
-    to_parts(g.part_c, g.hidden[...].reshape(512, D), lambda t: full_cols(g.full_d, t, 512), False, 3)
+    to_parts(g.pre_grad, lambda: g.hidden[...].reshape(512, D), lambda t: full_cols(g.full_d, t, 512), False, 3)
     scatter_u.first()
-    weight_grad(g.full_d, lambda t: g.hidden[:, :, cols(t, 384)].reshape(512, 384), up_all)
-    scatter_d = Both(lines, g.full_d, bufs("d"), 48, 768, D, True)
-    scatter_d.cores()
     ring_b.finish()
 
     grad_input[...] = grad_in[...].astype(F32) + rms_back(ring_b.total(g.part_a[x].astype(F32)), g.middle[...])
     g.branch[x] = grad_input[...].astype(BF)
     ring_g = gather_x(lines, lambda i, h: g.branch.at[i, h])
     ring_g.start()
+    weight_grad(g.full_d, lambda t: g.hidden[:, :, cols(t, 384)].reshape(512, 384), up_all)
+    scatter_d = scatter_both(lines, g.full_d, bufs("d"), 48, 768, D, True)
+    scatter_d.cores()
+    padded = pick(g.att[...].reshape(512, RANK_COLS), one_hot_rows(RANK_COLS, 512, False))
+    g.hidden[:, :, :512] = padded.reshape(4, 128, 512)
     scatter_u.on()
     ring_g.on()
     scatter_d.first()
     ring_g.finish()
-    ring_c = scatter_x(lines, g.part_c, g.got_c, g.via_c)
+    ring_c = scatter_x(lines, g.pre_grad, g.up_grad.at[:, LO], g.up_grad.at[pl.ds(0, 2), HI])
     ring_c.start()
 
-    branch_all = g.branch[...].reshape(512, D)
+    branch_all = lambda: g.branch[...].reshape(512, D)
     scatter_u.second()
-    g.att_grad[...] = dot_nt(branch_all, g.wo[...]).astype(BF).reshape(4, 128, RANK_COLS)
-    d_out = dot_tn(g.att[...].reshape(512, RANK_COLS), branch_all).astype(BF)
-    g.full_o[...] = pick(one_hot_rows(512, RANK_COLS, True), d_out).reshape(2, 2, 4, 32, D)
-    scatter_o = Both(lines, g.full_o, bufs("o"), 16, 768, D, True)
-    scatter_o.cores()
-
-    @pl.loop(0, RANK_HEADS)
-    def _(h):
+    g.att_grad[...] = dot_nt(branch_all(), g.wo[...]).astype(BF).reshape(4, 128, RANK_COLS)
+
+    def attend_back(h):
         at = pl.ds(pl.multiple_of(h * 128, 128), 128)
         g.dk_t[...] = jnp.zeros_like(g.dk_t)
         g.dv_t[...] = jnp.zeros_like(g.dv_t)
@@ -786,65 +836,78 @@
         g.k_ref[h] = dk.astype(BF).reshape(4, 2, 128, 128)
         g.v_ref[h] = g.dv_t[...].T.astype(BF).reshape(4, 2, 128, 128)
 
+    attend_back(0)
+    scatter_d.on()
+    pl.loop(1, RANK_HEADS)(attend_back)
     ring_c.on()
-    scatter_d.on()
-    scatter_o.first()
 
     def side(ref, zz):
         return [ref[h, :, zz].reshape(512, 128) for h in range(RANK_HEADS)]
 
     def first_parts(parts, zz, own_half):
-        pieces = side(g.k_ref, zz) + side(g.v_ref, zz)
-        if own_half:
-            pieces = [g.q_ref[h].reshape(512, 128) for h in range(RANK_HEADS)] + pieces
-        left = jnp.concatenate(pieces, axis=1)
-        n = left.shape[1]
+        def left():
+            pieces = side(g.k_ref, zz) + side(g.v_ref, zz)
+            if own_half:
+                pieces = [g.q_ref[h].reshape(512, 128) for h in range(RANK_HEADS)] + pieces
+            return jnp.concatenate(pieces, axis=1)
+
+        n = 1152 if own_half else 768
         to_parts(parts, left, lambda t: g.full_q[pl.ds(t * 2, 2), :, :, :, 1152 - n :].reshape(768, n), True, 2)
 
     first_parts(g.part_a, 1 - zh, False)
     ring_e = scatter_x(lines, g.part_a, g.got_a, g.via_a)
     ring_e.start()
-    first_parts(g.ntwo, zh, True)
-    ring_f = scatter_x(lines, g.ntwo, g.got_b, g.via_b)
-    ring_f.start()
-
-    dq_all = jnp.concatenate([g.q_ref[h].reshape(512, 128) for h in range(RANK_HEADS)], axis=1)
-    dkv_all = jnp.concatenate(
+    weight_grad(g.full_o, lambda t: g.hidden[:, :, cols(t, 128)].reshape(512, 128), branch_all)
+    scatter_o = scatter_both(lines, g.full_o, bufs("o"), 16, 768, D, True)
+    scatter_o.cores()
+    scatter_q = scatter_both(lines, g.full_u, bufs("q"), 48, RANK_COLS, 1152)
+    part_q, part_kv = scatter_q.parts
+    dq_all = lambda: jnp.concatenate([g.q_ref[h].reshape(512, 128) for h in range(RANK_HEADS)], axis=1)
+    dkv_all = lambda: jnp.concatenate(
         [r[h].reshape(GROUP, 128) for r in (g.k_ref, g.v_ref) for h in range(RANK_HEADS)], axis=1
     )
 
     @pl.loop(0, 4)
     def _(t):
-        mine = g.normed[:, zh, :, cols(t, 384)].reshape(512, 384)
         every = g.normed[:, :, :, cols(t, 384)].reshape(GROUP, 384)
-        g.full_u[t, :, :, :, :RANK_COLS] = dot_tn(mine, dq_all).astype(BF).reshape(2, 2, 96, RANK_COLS)
-        g.full_u[t, :, :, :, RANK_COLS:1152] = dot_tn(every, dkv_all).astype(BF).reshape(2, 2, 96, 768)
-
-    scatter_q = Both(lines, g.full_u, bufs("q"), 48, 640, 1152)
-    scatter_q.cores()
-    ring_e.on()
+        g.full_u[t, :, :, :, RANK_COLS:1152] = dot_tn(every, dkv_all()).astype(BF).reshape(2, 2, 96, 768)
+
+    part_kv.cores()
+    scatter_o.first()
     scatter_d.second()
-    scatter_q.first()
-    scatter_o.on()
-    ring_c.finish()
-    block_out[...] = ring_c.total(g.middle[...] + g.part_c[x].astype(F32)).astype(BF)
     spread_rows = one_hot_rows(64, 48, True)
     g.got_u[...] = pick(spread_rows, scatter_u.sums()).reshape(4, 16, D)
     plan_u = gather_home(lines, g.got_u, out_u)
     start_all(plan_u, g.got_u, out_u)
-    ring_f.on()
+
+    @pl.loop(0, 4)
+    def _(t):
+        mine = g.normed[:, zh, :, cols(t, 384)].reshape(512, 384)
+        g.full_u[t, :, :, :, :RANK_COLS] = dot_tn(mine, dq_all()).astype(BF).reshape(2, 2, 96, RANK_COLS)
+
+    part_q.cores()
+    part_kv.first()
+    ring_e.on()
+    part_q.first()
+    first_parts(g.ntwo, zh, True)
+    ring_f = scatter_x(lines, g.ntwo, g.got_b, g.via_b)
+    ring_f.start()
+    scatter_o.on()
     scatter_q.on()
     scatter_o.second()
+    g.down[...] = scatter_d.sums()
+    home_d = lines.copy(g.down, out_d, swap_xy())
+    home_o = lines.copy(g.src_o, out_o, swap_xy())
+    pl.when(x != y)(home_d.start)
     ring_e.finish()
-    g.swap_out[...] = ring_e.total(g.part_a[x].astype(F32)).astype(BF)
-    back = lines.copy(g.swap_out, g.swap_in, zh_peer())
+    g.grad_in[...] = ring_e.total(g.part_a[x].astype(F32)).astype(BF)
+    scatter_q.second()
+    back = lines.copy(g.grad_in, g.swap_in, zh_peer())
     back.start()
-    scatter_q.second()
-    g.fin_d[...] = scatter_d.sums()
-    home_d = lines.copy(g.fin_d, out_d, swap_xy())
-    home_o = lines.copy(g.fin_o, out_o, swap_xy())
-    pl.when(x != y)(home_d.start)
-    g.fin_o[...] = scatter_o.sums()
+    ring_f.on()
+    ring_c.finish()
+    block_out[...] = ring_c.total(g.middle[...] + g.pre_grad[x].astype(F32)).astype(BF)
+    g.src_o[...] = scatter_o.sums()
     pl.when(x != y)(home_o.start)
 
     g.got_q[...] = pick(spread_rows, scatter_q.sums()).reshape(4, 16, 1152)
@@ -857,8 +920,8 @@
 
     @pl.when(x == y)
     def _():
-        out_o[...] = g.fin_o[...]
-        out_d[...] = g.fin_d[...]
+        out_o[...] = g.src_o[...]
+        out_d[...] = g.down[...]
 
     wait_all(plan_u)
 
@@ -913,14 +976,14 @@
     made = pl.pallas_call(
         layer_kernel,
         out_shape=shapes_of(outs),
-        in_specs=[smem] * 2 + [vmem] * 9,
+        in_specs=[smem] * 2 + [vmem] * 2 + [pl.BlockSpec(memory_space=pl.ANY)] * 7,
         out_specs=[vmem] * len(outs),
         scratch_shapes=scratch_list(),
         compiler_params=pltpu.CompilerParams(collective_id=0, has_side_effects=True, vmem_limit_bytes=VMEM_LIMIT),
         name="layer_kernel",
     )(
-        doc_lengths, ffn_levels, block_input[0], grad_output[0], qkv_weight, out_weight, up_weight, down_weight,
-        gain_one, gain_two, jnp.asarray(tables()),
+        doc_lengths, ffn_levels, gain_one, gain_two, block_input[0], grad_output[0], qkv_weight, out_weight, up_weight,
+        down_weight, jnp.asarray(tables()),
     )
     outs = [((128, D), BF), ((128, D), F32), ((1, 12), F32), ((12, 3 * D), F32), ((12, D), F32), ((1, 12), F32)]
     outs += [((12, FF), F32), ((48, D), F32)]

time: 199 us -> 185 us (0.930); the launches traced: 196 us -> 185 us
  Pallas kernels: 196 us -> 184 us
    pallas_call x1, Pallas kernels: 193 us -> 181 us  [per_device(): pl.pallas_call(layer_kernel, out_shape=shapes_of(outs), in_specs=[smem] *...]
where the time goes in v2:
time: 185 us
  Pallas kernels  184 us (99%)
    pallas_call x1, Pallas kernels, per_device(): pl.pallas_call(layer_kernel, out_shape=shapes_of(outs), in_specs=[smem] *...  181 us

profile of v2, /device:TPU:0, one launch (start us, length us, event | category | flops | bytes accessed | tf_op | source)
XLA Modules:
  0.0 184.7 jit_solution(6156181130457225346)
XLA Ops:
  0.6 181.0 %layer_kernel.1 = (bf16[128,1536]{1,0:T(8,128)(2,1)}, f32[128,1536]{1,0:T(8,128)}, bf16[4,16,1152]{2,1,0:T(8,128)(2,1)}, bf16[4,16,1536]{2,1,0:T(8,128)(2,1)}, b...) custom-call(s32[1,6]{1,0:T(1,128)} %lengths.1, s32[1,6]{1,0:T(1,128)} %levels.1, bf16[1,12]{1,0:T(2,128)(2,1)} %bitcast.10, ...), custom_call_target="tpu_custom_call" | custom-call | tf_op jit(solution)/shard_map/layer_kernel/pallas_call | solution.py:976
  181.6 3.1 %finish_kernel.1 = (bf16[128,1536]{1,0:T(8,128)(2,1)}, f32[128,1536]{1,0:T(8,128)}, f32[1,12]{1,0:T(1,128)}, f32[12,4608]{1,0:T(8,128)}, f32[12,1536]{1,0:T(8,12...) custom-call(bf16[128,1536]{1,0:T(8,128)(2,1)} %get-tuple-element.22.block, ...), custom_call_target="tpu_custom_call" | custom-call | tf_op jit(solution)/shard_map/finish_kernel/pallas_call | solution.py:990

commit v3 on v2

--- a/solution.py
+++ b/solution.py
@@ -429,8 +429,8 @@
 
 def gather_both(lines, full, rows, split, width, y_inner=False):
     return Pair(
+        Gather(lines, full, rows, False, y_inner, pl.ds(split, width - split)),
         Gather(lines, full, rows, True, y_inner, pl.ds(0, split)),
-        Gather(lines, full, rows, False, y_inner, pl.ds(split, width - split)),
     )
 
 
@@ -638,9 +638,9 @@
     gather_q.on()
     pl.when(x != y)(swap_o.wait)
     gather_o.near()
+    ring_two.on()
     plan_u = spread(lines, g.src_u, g.got_u)
     start_all(plan_u, g.src_u, g.got_u)
-    ring_two.on()
     gather_q.cores()
     gather_o.wide()
     pl.when(x != y)(swap_d.wait)
@@ -667,15 +667,15 @@
 
     project(zh, True)
     gather_o.on()
-    gather_d.wide()
-    wait_all(plan_u)
-    g.full_u[y, zl, c, pl.ds(zh * 48, 48)] = pick(rows, g.got_u[...].reshape(64, D))
-    gather_u.near()
     ring_two.finish()
     swap.wait_send()
     ring_up = gather_x(lines, lambda i, h: g.up_grad.at[i, h])
     ring_up.start()
     project(1 - zh, False)
+    gather_d.wide()
+    wait_all(plan_u)
+    g.full_u[y, zl, c, pl.ds(zh * 48, 48)] = pick(rows, g.got_u[...].reshape(64, D))
+    gather_u.near()
     gather_o.cores()
 
     probs = [g.p0, g.p1, g.p2, g.p3]
@@ -697,9 +697,10 @@
             g.att[i, :, pl.ds(pl.multiple_of(h * 128, 128), 128)] = dot(p, values).astype(BF)
 
     attend(0)
+    ring_up.on()
+    attend(1)
     gather_d.on()
-    ring_up.on()
-    pl.loop(1, RANK_HEADS)(attend)
+    attend(2)
     gather_o.wait()
     g.wo[...] = pick(one_hot_rows(RANK_COLS, 512, False), g.full_o[...].reshape(512, D))
 
@@ -718,10 +719,10 @@
     gather_u.wide()
     gather_d.cores()
 
+    ring_a.on()
     gather_u.on()
     ring_up.finish()
     gather_d.wait()
-    ring_a.on()
     up_all = lambda: g.up_grad[...].reshape(512, D)
     to_parts(g.pre_grad, up_all, lambda t: g.full_d[t].reshape(768, D), True, 2)
     gather_u.cores()

time: 185 us -> 183 us (0.989)
  Pallas kernels: 184 us -> 181 us
    pallas_call x1, Pallas kernels: 181 us -> 178 us  [per_device(): pl.pallas_call(layer_kernel, out_shape=shapes_of(outs), in_specs=[smem] *...]
where the time goes in v3:
time: 183 us; the launch traced here: 182 us
  Pallas kernels  181 us (99%)
    pallas_call x1, Pallas kernels, per_device(): pl.pallas_call(layer_kernel, out_shape=shapes_of(outs), in_specs=[smem] *...  178 us

profile of v3, /device:TPU:0, one launch (start us, length us, event | category | flops | bytes accessed | tf_op | source)
XLA Modules:
  0.0 181.9 jit_solution(10417671514668146940)
XLA Ops:
  0.6 178.2 %layer_kernel.1 = (bf16[128,1536]{1,0:T(8,128)(2,1)}, f32[128,1536]{1,0:T(8,128)}, bf16[4,16,1152]{2,1,0:T(8,128)(2,1)}, bf16[4,16,1536]{2,1,0:T(8,128)(2,1)}, b...) custom-call(s32[1,6]{1,0:T(1,128)} %lengths.1, s32[1,6]{1,0:T(1,128)} %levels.1, bf16[1,12]{1,0:T(2,128)(2,1)} %bitcast.10, ...), custom_call_target="tpu_custom_call" | custom-call | tf_op jit(solution)/shard_map/layer_kernel/pallas_call | solution.py:977
  178.9 3.1 %finish_kernel.1 = (bf16[128,1536]{1,0:T(8,128)(2,1)}, f32[128,1536]{1,0:T(8,128)}, f32[1,12]{1,0:T(1,128)}, f32[12,4608]{1,0:T(8,128)}, f32[12,1536]{1,0:T(8,12...) custom-call(bf16[128,1536]{1,0:T(8,128)(2,1)} %get-tuple-element.22.block, ...), custom_call_target="tpu_custom_call" | custom-call | tf_op jit(solution)/shard_map/finish_kernel/pallas_call | solution.py:991
